TPU v7x, 768 devices: a whole 4x8x12 slice. The times are simulated.
768 devices in a mesh: dp: 12 (over x, z_hi), tensor: 64 (over y, z_lo, core).
Axes of the slice: x: 4, y: 8, z: 12 (z_hi: 3, z_lo: 4; z = z_hi * 4 + z_lo), core: 2. Of those that a mesh axis runs over, the one named last changes fastest.
Arguments:
- tokens: bfloat16 [3072, 4096], P(('dp', 'tensor')), may hold values from -6 to 6
- norm_gain: bfloat16 [4096], replicated, may hold values from 0.099609375 to 1.8984375
- gate_weight: bfloat16 [4096, 14336], P(None, 'tensor'), may hold values from -0.09375 to 0.09375
- up_weight: bfloat16 [4096, 14336], P(None, 'tensor'), may hold values from -0.09375 to 0.09375
- down_weight: bfloat16 [14336, 4096], P('tensor'), may hold values from -0.046875 to 0.046875
- drop_mask: int32 [3072, 4096], P(('dp', 'tensor')), may hold values 0 or 1
- grad_bucket: bfloat16 [12, 16384, 1536], P('dp', 'tensor'), may hold values from -6 to 6
Outputs:
- mixed: bfloat16 [3072, 4096], P(('dp', 'tensor'))
- reduced: float32 [16384, 1536], P('tensor', 'dp')
All inputs are finite; a program needn't handle non-finite values. No bound on the sum of `drop_mask` on one device may be relied on, other than what follows from the above.
Results may differ from a plain program's by a relative error of at most 0.012.
Values may be sent and summed in bfloat16 or wider, within the bound.
No kernel may reach another device: no remote copies, remote signals or barrier semaphores. Data moves between devices by JAX's collectives and lax.ppermute only.
A program may use at most 64 MiB of HBM per device.

v0:
```python
import jax
import jax.numpy as jnp
from jax import lax
from jax.sharding import Mesh
from jax.sharding import PartitionSpec as P

DP = ("dp_0", "dp_1")
TENSOR = ("tensor_0", "tensor_1", "tensor_2")
DP_TENSOR = ("dp_0", "dp_1", "tensor_0", "tensor_1", "tensor_2")


def summed_rows(x, axes, dim):
    for axis in axes:
        x = lax.psum_scatter(x, axis, scatter_dimension=dim, tiled=True)
    return x


def in_order(pieces, dim):
    pieces = jnp.moveaxis(pieces, 0, dim)
    shape = pieces.shape
    return pieces.reshape(*shape[:dim], shape[dim] * shape[dim + 1], *shape[dim + 2 :])


def copy_for_each(x, axis):
    size = lax.axis_size(axis)
    return lax.all_to_all(jnp.broadcast_to(x[None], (size, *x.shape)), axis, 0, 0, tiled=True)


def gathered_copies(x, axis, dim):
    return in_order(copy_for_each(x, axis), dim)


def in_blocks(x, dim, size):
    before, after = (x.shape[:dim], x.shape[dim + 1 :])
    return jnp.moveaxis(x.reshape(*before, size, -1, *after), dim, 0)


def scatter_pairs(x, chips, core, dim):
    sizes = (lax.axis_size(chips), lax.axis_size(core))
    pieces = in_blocks(x, dim, sizes[0] * sizes[1])
    inside = pieces.shape[1:]
    pieces = pieces.reshape(*sizes, *inside).swapaxes(0, 1).reshape(-1, *inside)
    pieces = lax.psum_scatter(pieces, core, scatter_dimension=0, tiled=True)
    return lax.psum_scatter(pieces, chips, scatter_dimension=0, tiled=True)[0]


def per_device(tokens, norm_gain, gate_weight, up_weight, down_weight, drop_mask, grad_bucket):
    reduced = summed_rows(grad_bucket[0].astype(jnp.float32).astype(jnp.bfloat16), DP, 1).astype(
        jnp.float32
    )
    inputs = tokens.astype(jnp.float32)
    scale = lax.rsqrt(jnp.mean(inputs * inputs, axis=-1, keepdims=True) + 1e-05)
    normed = (inputs * scale * norm_gain.astype(jnp.float32)).astype(jnp.bfloat16)
    gathered = gathered_copies(normed, TENSOR, 0)
    gate = jnp.dot(gathered, gate_weight, preferred_element_type=jnp.float32)
    up_part = jnp.dot(gathered, up_weight, preferred_element_type=jnp.float32)
    hidden = (jax.nn.silu(gate) * up_part).astype(jnp.bfloat16)
    partial_terms = jnp.dot(hidden, down_weight, preferred_element_type=jnp.float32)
    branch = scatter_pairs(partial_terms, ("tensor_0", "tensor_1"), "tensor_2", 0)
    mixed = (inputs + drop_mask.astype(jnp.float32) * branch / 0.9).astype(jnp.bfloat16)
    return (mixed, reduced)


def solution(mesh):
    finer = Mesh(
        mesh.devices.reshape(4, 3, 8, 4, 2), ("dp_0", "dp_1", "tensor_0", "tensor_1", "tensor_2")
    )
    return jax.shard_map(
        per_device,
        mesh=finer,
        in_specs=(
            P(DP_TENSOR, None),
            P(),
            P(None, TENSOR),
            P(None, TENSOR),
            P(TENSOR, None),
            P(DP_TENSOR, None),
            P(DP, TENSOR, None),
        ),
        out_specs=(P(DP_TENSOR, None), P(TENSOR, DP)),
        check_vma=False,
    )
```

profile of v0, /device:TPU:6, one launch (start us, length us, event | category | flops | bytes accessed | tf_op | source)
XLA Modules:
  0.0 491.0 jit_solution(15396390898983474588)
XLA Ops:
  8.0 0.0 copy-start
  8.0 0.8 convert_element_type.25
  8.8 0.9 fusion.8
  9.8 0.8 fusion.10
  10.6 2.3 broadcast_in_dim.2
  12.9 0.0 copy-start.1
  12.9 13.9 %all-to-all-start = ((bf16[64,4,4096]{2,1,0:T(4,128)(2,1)}), bf16[64,4,4096]{2,1,0:T(4,128)(2,1)}, u32[]{:S(2)}, u32[]{:S(2)}) async-start(bf16[64,4,4096]{2,1,0:T(4,128)(2,1)} %broadcast_in_dim.2), calls=%async_computation | async-start | bytes 4194304 | tf_op jit(solution)/shard_map/all_to_all | solution.py:26
  26.9 0.0 reduce-scatter.7.cloned.1.call-start
  26.9 0.0 copy-done.1
  26.9 1.2 copy.11
  28.1 0.0 reduce-scatter.7.cloned.1.call-update
  28.2 0.0 all-reduce.5.cloned.1.call-start
  28.2 50.9 %all-to-all-done = bf16[64,4,4096]{2,1,0:T(4,128)(2,1)} async-done(((bf16[64,4,4096]{2,1,0:T(4,128)(2,1)}), bf16[64,4,4096]{2,1,0:T(4,128)(2,1)}, u32[]{:S(2)}, u32[]{:S(2)}) %all-to-all-start) | async-done | bytes 2097184 | tf_op jit(solution)/shard_map/all_to_all | solution.py:26
  79.1 4.0 reshape.20
  83.1 2.9 fusion.15
  86.0 0.0 copy-done
  86.0 6.6 %fusion.1 = f32[256,4096]{1,0:T(8,128)} fusion(bf16[224,4096]{1,0:T(8,128)(2,1)S(1)} %copy-done, bf16[256,4096]{1,0:T(8,128)(2,1)} %reshape.20, bf16[4096,224]{0,1:T(8,128)(2,1)} %param.10, f32[256,224]{0,1:T(8,128)S(1)} %fusion.15), kind=kOutput, calls=%fused_computation.2 | convolution fusion | flops 939868160 | bytes 10190848 | tf_op jit(solution)/shard_map/dot_general | solution.py:58
  92.6 5.2 %reshape_reshape.3 = f32[32,2,4,4096]{3,2,1,0:T(4,128)} reshape(f32[256,4096]{1,0:T(8,128)} %fusion.1) | data formatting | bytes 8388608 | tf_op jit(solution)/shard_map/reshape;reshape | solution.py:42
  97.8 4.7 copy.10
  102.4 0.0 all-reduce.5.cloned.1.call-update
  102.5 0.0 reduce-scatter.9.cloned.1.call-start
  102.5 1.3 dynamic-slice
  104.4 0.0 reduce-scatter.7.cloned.1.call-done
  104.5 0.0 reduce-scatter.9.cloned.1.call-update
  104.5 0.0 all-reduce.7.cloned.1.call-start
  104.5 46.7 %all-reduce.5.cloned.1.call-done = f32[64,4,4096]{2,1,0:T(4,128)} async-done(((f32[64,4,4096]{2,1,0:T(4,128)}), f32[64,4,4096]{2,1,0:T(4,128)}) %all-reduce.5.cloned.1.call-update) | async-done | bytes 4194320
  151.2 3.1 constant_dynamic-slice_fusion
  154.3 0.0 copy-start.2
  154.3 0.0 copy-start.3
  154.3 0.0 all-reduce.7.cloned.1.call-update
  154.4 1.4 dynamic-slice.2
  155.7 0.0 reduce-scatter.9.cloned.1.call-done
  155.7 0.9 copy.14
  156.7 0.7 convert_element_type.29
  157.4 324.1 %all-reduce.7.cloned.1.call-done = f32[32,4,4096]{2,1,0:T(4,128)} async-done(((f32[32,4,4096]{2,1,0:T(4,128)}), f32[32,4,4096]{2,1,0:T(4,128)}) %all-reduce.7.cloned.1.call-update) | async-done | bytes 2097168
  481.4 0.0 copy-done.2
  481.4 0.0 copy-done.3
  481.4 2.1 fusion.11
  (1 shorter events, 0.0 us)
Async XLA Ops:
  8.0 78.0 %copy-start = (bf16[224,4096]{1,0:T(8,128)(2,1)S(1)}, bf16[224,4096]{1,0:T(8,128)(2,1)}, u32[]{:S(2)}) copy-start(bf16[224,4096]{1,0:T(8,128)(2,1)} %param.11) | copy-start | bytes 5505028
  12.9 14.0 %copy-start.1 = (bf16[1,256,1536]{2,1,0:T(8,128)(2,1)S(1)}, bf16[1,256,1536]{2,1,0:T(8,128)(2,1)}, u32[]{:S(2)}) copy-start(bf16[1,256,1536]{2,1,0:T(8,128)(2,1)} %param.13) | copy-start | bytes 2359300
  12.9 66.2 %all-to-all-start = ((bf16[64,4,4096]{2,1,0:T(4,128)(2,1)}), bf16[64,4,4096]{2,1,0:T(4,128)(2,1)}, u32[]{:S(2)}, u32[]{:S(2)}) async-start(bf16[64,4,4096]{2,1,0:T(4,128)(2,1)} %broadcast_in_dim.2), calls=%async_computation | async-start | bytes 4194304 | tf_op jit(solution)/shard_map/all_to_all | solution.py:26
  26.9 77.6 %reduce-scatter.7.cloned.1.call-start = ((), (), s32[]{:S(2)}) async-start(), calls=%async_computation.3 | async-start | bytes 983040
  28.2 123.0 %all-reduce.5.cloned.1.call-start = ((), (), s32[]{:S(2)}) async-start(), calls=%async_computation.5 | async-start | bytes 8388608
  102.5 53.3 %reduce-scatter.9.cloned.1.call-start = ((), (), s32[]{:S(2)}) async-start(), calls=%async_computation.4 | async-start | bytes 262144
  104.5 376.9 %all-reduce.7.cloned.1.call-start = ((), (), s32[]{:S(2)}) async-start(), calls=%async_computation.6 | async-start | bytes 4194304
  154.3 327.1 %copy-start.2 = (bf16[4,4096]{1,0:T(4,128)(2,1)S(1)}, bf16[4,4096]{1,0:T(4,128)(2,1)}, u32[]{:S(2)}) copy-start(bf16[4,4096]{1,0:T(4,128)(2,1)} %param.7) | copy-start | bytes 98308
  154.3 327.1 %copy-start.3 = (s32[4,4096]{1,0:T(4,128)S(1)}, s32[4,4096]{1,0:T(4,128)}, u32[]{:S(2)}) copy-start(s32[4,4096]{1,0:T(4,128)} %param.12) | copy-start | bytes 196612
Sparse Core Ops, SparseCore 0:
  30.9 32.7 reduce-scatter.6
  106.4 31.7 reduce-scatter.8
Sparse Core Ops, SparseCore 1:
  102.5 48.6 all-reduce.4
  154.6 326.8 all-reduce.6
where the time goes:
time: 492 us; the launch traced here: 491 us
  waiting for transfers between devices  422 us (86%)
  local copies, waits for them, and re-layouts  24 us (5%)
  between operations  16.2 us (3%)
  starting transfers between devices  14.1 us (3%)
  matrix products  9.49 us (2%)
  other arithmetic  5.37 us (1%)
    unnamed x8, waiting for transfers between devices  371 us
    all_to_all x1, waiting for transfers between devices, copy_for_each(): lax.all_to_all(jnp.broadcast_to(x[None], (size, *x.shape)), axis, 0, 0, t...  50.9 us
    all_to_all x1, starting transfers between devices, copy_for_each(): lax.all_to_all(jnp.broadcast_to(x[None], (size, *x.shape)), axis, 0, 0, t...  13.9 us
  transfers between devices with their start and end apart: 5, of which 3 were waited for; matrix products, arithmetic and copies ran while one was open for 6% of the time, Pallas kernels for 0%

commit v1 on v0

v1 whole, which is shorter than its diff:
```python
import functools

import jax
import jax.numpy as jnp
from jax import lax
from jax.experimental import pallas as pl
from jax.experimental.pallas import tpu as pltpu
from jax.sharding import Mesh
from jax.sharding import PartitionSpec as P

DP = ("x", "zh")
TENSOR = ("y", "zl", "c")
BF16, F32 = jnp.bfloat16, jnp.float32
EPS = 1e-05
KEEP = 0.9


def call(body, outs, *args, smem=0, scratch=(), vmem=32, flops=0, moved=1 << 20):
    whole = pl.BlockSpec(memory_space=pltpu.VMEM)
    return pl.pallas_call(
        body,
        out_shape=outs,
        in_specs=[pl.BlockSpec(memory_space=pltpu.SMEM)] * smem + [whole] * (len(args) - smem),
        out_specs=jax.tree.map(lambda _: whole, outs),
        scratch_shapes=list(scratch),
        compiler_params=pltpu.CompilerParams(vmem_limit_bytes=vmem << 20),
        cost_estimate=pl.CostEstimate(flops=flops, bytes_accessed=moved, transcendentals=0),
    )(*args)


def norm_body(tok_ref, gain_ref, out_ref):
    few, wide = tok_ref.shape
    quarter = wide // 4
    inputs = tok_ref[...].astype(F32)
    scale = lax.rsqrt(jnp.mean(inputs * inputs, axis=-1, keepdims=True) + EPS)
    normed = inputs * scale * gain_ref[...].astype(F32)
    for half in range(2):
        at = 2 * half * quarter
        block = jnp.concatenate(
            [normed[:, at : at + quarter], normed[:, at + quarter : at + 2 * quarter]], axis=0
        ).astype(BF16)
        for i in range(out_ref.shape[0] // 2):
            out_ref[2 * i + half] = block


def paired(first, second):
    upper = lax.broadcasted_iota(jnp.int32, first.shape, 1) < first.shape[1] // 2
    turn = first.shape[1] // 2
    return (
        jnp.where(upper, first, pltpu.roll(second, turn, 1)),
        jnp.where(upper, pltpu.roll(first, turn, 1), second),
    )


def dot_t(x, w):
    return lax.dot_general(x, w, (((1,), (1,)), ((), ())), preferred_element_type=F32)


def halves(x_ref):
    blocks, eight, quarter = x_ref.shape
    x = x_ref[...].astype(F32).reshape(blocks // 2, 2, eight, quarter)
    first, second = paired(x[:, 0], x[:, 1])
    rows = blocks * eight // 2
    return first.reshape(rows, quarter).astype(BF16), second.reshape(rows, quarter).astype(BF16)


def lead_body(core_ref, x_ref, gate_ref, up_ref, gate_out, up_out):
    quarter = x_ref.shape[-1]
    at = pl.multiple_of(core_ref[0] * (2 * quarter), 2 * quarter)
    first, second = halves(x_ref)
    for w_ref, out in ((gate_ref, gate_out), (up_ref, up_out)):
        part = dot_t(first, w_ref[:, pl.ds(at, quarter)])
        out[...] = part + dot_t(second, w_ref[:, pl.ds(at + quarter, quarter)])


def hidden_body(core_ref, x_ref, gate_ref, up_ref, down_ref, gate_in, up_in, hid_out, far_out):
    quarter = x_ref.shape[-1]
    at = pl.multiple_of((1 - core_ref[0]) * (2 * quarter), 2 * quarter)
    first, second = halves(x_ref)

    def both(w_ref, part_ref):
        part = part_ref[...] + dot_t(first, w_ref[:, pl.ds(at, quarter)])
        return part + dot_t(second, w_ref[:, pl.ds(at + quarter, quarter)])

    gate = both(gate_ref, gate_in)
    up = both(up_ref, up_in)
    hidden = (gate / (1.0 + jnp.exp(-gate)) * up).astype(BF16)
    hid_out[...] = hidden
    for k in range(4):
        cols = pl.ds(at + k * (quarter // 2), quarter // 2)
        out = jnp.dot(hidden, down_ref[:, cols], preferred_element_type=F32)
        far_out[:, k * (quarter // 2) : (k + 1) * (quarter // 2)] = out.astype(BF16)


def down_body(core_ref, hid_ref, down_ref, near_ref, out_ref):
    blocks, eight, quarter = out_ref.shape
    at = pl.multiple_of(core_ref[0] * (2 * quarter), 2 * quarter)
    hidden = hid_ref[...]
    step = quarter // 2
    for k in range(2):
        sums = []
        for q in range(2):
            here = q * quarter + k * step
            part = jnp.dot(hidden, down_ref[:, pl.ds(at + here, step)], preferred_element_type=F32)
            part += near_ref[:, here : here + step].astype(F32)
            sums.append(part.reshape(blocks // 2, eight, step))
        both = jnp.stack(paired(*sums), axis=1)
        out_ref[:, :, k * step : (k + 1) * step] = both.reshape(blocks, eight, step).astype(BF16)


def final_body(in_ref, tok_ref, mask_ref, out_ref):
    few, wide = tok_ref.shape
    quarter = wide // 4
    for half in range(2):
        total = in_ref[half].astype(F32)
        for i in range(1, in_ref.shape[0] // 2):
            total = total + in_ref[2 * i + half].astype(F32)
        for q in range(2):
            cols = slice((2 * half + q) * quarter, (2 * half + q + 1) * quarter)
            branch = total[q * few : (q + 1) * few]
            kept = mask_ref[:, cols].astype(F32) * branch / KEEP
            out_ref[:, cols] = (tok_ref[:, cols].astype(F32) + kept).astype(BF16)


def cut_body(place_ref, in_ref, *outs):
    width = outs[0].shape[1]
    for k, out in enumerate(outs):
        at = lax.rem(place_ref[0] + k, len(outs)) * width
        out[...] = in_ref[:, pl.ds(pl.multiple_of(at, width), width)]


def sum_cut_body(place_ref, *refs, terms):
    total = refs[0][...].astype(F32)
    for ref in refs[1:terms]:
        total = total + ref[...].astype(F32)
    outs, held = refs[terms:-1], refs[-1]
    held[...] = total
    width = outs[0].shape[1]
    for k, out in enumerate(outs):
        at = lax.rem(place_ref[0] + k, len(outs)) * width
        out[...] = held[:, pl.ds(pl.multiple_of(at, width), width)].astype(out.dtype)


def sum_body(*refs):
    total = refs[0][...].astype(F32)
    for ref in refs[1:-1]:
        total = total + ref[...].astype(F32)
    refs[-1][...] = total


def shape(*dims, dtype=BF16):
    return jax.ShapeDtypeStruct(dims, dtype)


def place(axis):
    return lax.axis_index(axis).astype(jnp.int32).reshape(1)


def passed_on(x, axis, by):
    size = lax.axis_size(axis)
    return lax.ppermute(x, axis, [(i, (i + by) % size) for i in range(size)])


def bucket_sum(bucket):
    rows, cols = bucket.shape
    nx, nh = lax.axis_size("x"), lax.axis_size("zh")
    wide, narrow = cols // nx, cols // nx // nh
    cut = call(cut_body, (shape(rows, wide),) * nx, place("x"), bucket, smem=1)
    terms = [cut[0]] + [passed_on(cut[k], "x", k) for k in range(1, nx)]
    cut = call(
        functools.partial(sum_cut_body, terms=nx),
        (shape(rows, narrow),) * nh,
        place("zh"), *terms,
        smem=1, scratch=[pltpu.VMEM((rows, wide), F32)],
    )
    terms = [cut[0]] + [passed_on(cut[k], "zh", k) for k in range(1, nh)]
    return call(sum_body, shape(rows, narrow, dtype=F32), *terms)


def per_device(tokens, norm_gain, gate_weight, up_weight, down_weight, drop_mask, grad_bucket):
    few, wide = tokens.shape
    quarter = wide // 4
    group = lax.axis_size(TENSOR)
    rows = group * few
    units = gate_weight.shape[1]
    core = place("c")
    gate_weight, up_weight = gate_weight.T, up_weight.T
    blocks = shape(group, 2 * few, quarter)
    part = shape(rows, units, dtype=F32)

    reduced = bucket_sum(grad_bucket[0])

    own = call(norm_body, blocks, tokens, norm_gain.reshape(1, wide))
    own = lax.all_to_all(own, TENSOR, 0, 0, tiled=True)
    far = passed_on(own, "c", 1)
    gate, up = call(
        lead_body, (part, part), core, own, gate_weight, up_weight,
        smem=1, flops=2 * rows * wide * units,
    )
    hidden, send = call(
        hidden_body,
        (shape(rows, units), shape(rows, 2 * quarter)),
        core, far, gate_weight, up_weight, down_weight, gate, up,
        smem=1, flops=3 * rows * wide * units,
    )
    near = passed_on(send, "c", 1)
    terms = call(down_body, blocks, core, hidden, down_weight, near, smem=1, flops=rows * wide * units)
    terms = lax.all_to_all(terms, TENSOR, 0, 0, tiled=True)
    mixed = call(final_body, shape(few, wide), terms, tokens, drop_mask)
    return (mixed, reduced)


def solution(mesh):
    finer = Mesh(mesh.devices.reshape(4, 3, 8, 4, 2), DP + TENSOR)
    return jax.shard_map(
        per_device,
        mesh=finer,
        in_specs=(
            P(DP + TENSOR, None),
            P(),
            P(None, TENSOR),
            P(None, TENSOR),
            P(TENSOR, None),
            P(DP + TENSOR, None),
            P(DP, TENSOR, None),
        ),
        out_specs=(P(DP + TENSOR, None), P(TENSOR, DP)),
        check_vma=False,
    )
```

time: 492 us -> 107 us (0.22)
  the two profiles are of different devices: /device:TPU:6 before, /device:TPU:10 now
where the time goes in v1:
time: 107 us; the launch traced here: 106 us
  blocking collectives  41.8 us (39%)
  starting transfers between devices  34.9 us (33%)
  waiting for transfers between devices  19.1 us (18%)
  Pallas kernels  6.5 us (6%)
  local copies, waits for them, and re-layouts  3.37 us (3%)
    all_to_all x1, blocking collectives, per_device(): own = lax.all_to_all(own, TENSOR, 0, 0, tiled=True)  41.8 us
    ppermute x7, starting transfers between devices, passed_on(): return lax.ppermute(x, axis, [(i, (i + by) % size) for i in range(size)])  28.6 us
    ppermute x7, waiting for transfers between devices, passed_on(): return lax.ppermute(x, axis, [(i, (i + by) % size) for i in range(size)])  19.1 us
    pallas_call x8, Pallas kernels, call(): pl.pallas_call(body, out_shape=outs, in_specs=[pl.BlockSpec(memory_space=...  6.5 us
    all_to_all x1, starting transfers between devices, per_device(): terms = lax.all_to_all(terms, TENSOR, 0, 0, tiled=True)  6.33 us
    unnamed x14, local copies, waits for them, and re-layouts  2.52 us
  transfers between devices with their start and end apart: 8, of which 6 were waited for; matrix products, arithmetic and copies ran while one was open for 0% of the time, Pallas kernels for 2%

profile of v1, /device:TPU:10, one launch (start us, length us, event | category | flops | bytes accessed | tf_op | source)
XLA Modules:
  0.0 106.4 jit_solution(3023193662448926836)
XLA Ops:
  0.6 0.0 copy-start
  0.6 0.8 reshape.17.gain_ref
  1.5 0.0 copy-start.4
  1.5 0.7 copy-done.4
  2.2 0.2 shard_map.86
  2.4 41.8 %all_to_all.10.x_ref = bf16[64,8,1024]{2,1,0:T(8,128)(2,1)S(1)} all-to-all(bf16[64,8,1024]{2,1,0:T(8,128)(2,1)S(1)} %shard_map.86), channel_id=1, replica_groups=mesh['x'=4,'zh'=3,'y'=8,'zl'=4,'c'=2] {'y','zl','c'}, dimensions={0} | all-to-all | bytes 2097152 | tf_op jit(solution)/shard_map/all_to_all | solution.py:194
  44.2 1.9 %collective-permute-start = (bf16[64,8,1024]{2,1,0:T(8,128)(2,1)S(1)}, bf16[64,8,1024]{2,1,0:T(8,128)(2,1)}, u32[]{:S(2)}, u32[]{:S(2)}) collective-permute-start(bf16[64,8,1024]{2,1,0:T(8,128)(2,1)S(1)} %all_to_all.10.x_ref), channel_id=1, source_target_pairs={{0,1},{1,0},{2,3},{3,2},{4,5},{5,4},{6,7},{7,6},{8,9},{9,8},{10,11... | collective-permute-start | bytes 3145736 | tf_op jit(solution)/shard_map/ppermute | solution.py:161
  46.2 0.0 copy-done
  46.2 0.0 copy-start.1
  46.2 1.5 %copy-done.1 = bf16[4096,224]{0,1:T(8,128)(2,1)S(1)} copy-done((bf16[4096,224]{0,1:T(8,128)(2,1)S(1)}, bf16[4096,224]{0,1:T(8,128)(2,1)}, u32[]{:S(2)}) %copy-start.1) | copy-done | bytes 1835032
  47.7 0.0 copy-start.2
  47.7 0.7 shard_map.87
  48.4 0.5 collective-permute-done.x_ref
  48.9 0.3 copy-done.2
  49.2 2.4 %shard_map.88 = (bf16[256,224]{1,0:T(8,128)(2,1)S(1)}, bf16[256,2048]{1,0:T(8,128)(2,1)S(1)}) custom-call(s32[1]{0:T(128)} %bitcast.core_ref, bf16[64,8,1024]{2,1,0:T(8,128)(2,1)} %collective-permute-done.x_ref, bf16[224,4096]{1,0:T(8,128)(2,1)S(1)} %bitcast.7, bf16[224,4096]{1,0:T(8,128)(2,1)S(1)} %bitcast.9, bf16[224,4096]{1,0:T(8,128)(2,1)S(1)} %copy-done.2, ...), custom_call_target="tpu_custom_call" | custom-call | flops 704643072 | bytes 1048576 | tf_op jit(solution)/shard_map/pallas_call | solution.py:20
  51.6 2.4 %collective-permute-start.1 = (bf16[256,2048]{1,0:T(8,128)(2,1)S(1)}, bf16[256,2048]{1,0:T(8,128)(2,1)S(1)}, u32[]{:S(2)}, u32[]{:S(2)}) collective-permute-start(bf16[256,2048]{1,0:T(8,128)(2,1)S(1)} %get-tuple-element.16), channel_id=1, source_target_pairs={{0,1},{1,0},{2,3},{3,2},{4,5},{5,4},{6,7},{7,6},{8,9},{9,8},{10,11... | collective-permute-start | bytes 3145736 | tf_op jit(solution)/shard_map/ppermute | solution.py:161
  54.0 2.3 %collective-permute-done.1.near_ref = bf16[256,2048]{1,0:T(8,128)(2,1)S(1)} collective-permute-done((bf16[256,2048]{1,0:T(8,128)(2,1)S(1)}, bf16[256,2048]{1,0:T(8,128)(2,1)S(1)}, u32[]{:S(2)}, u32[]{:S(2)}) %collective-permute-start.1) | collective-permute-done | bytes 1048608 | tf_op jit(solution)/shard_map/ppermute | solution.py:161
  56.2 1.5 %shard_map.89 = bf16[64,8,1024]{2,1,0:T(8,128)(2,1)} custom-call(s32[1]{0:T(128)} %bitcast.core_ref, bf16[256,224]{1,0:T(8,128)(2,1)S(1)} %get-tuple-element.15.hid_ref, bf16[224,4096]{1,0:T(8,128)(2,1)S(1)} %copy-done.2, bf16[256,2048]{1,0:T(8,128)(2,1)S(1)} %collective-permute-done.1.near_ref), custom_call_target="tpu_custom_call" | custom-call | flops 234881024 | bytes 1048576 | tf_op jit(solution)/shard_map/pallas_call | solution.py:20
  57.8 0.0 copy-start.3
  57.8 0.0 copy-start.5
  57.8 0.0 copy-start.6
  57.8 6.3 %all-to-all-start.1 = ((bf16[64,8,1024]{2,1,0:T(8,128)(2,1)}), bf16[64,8,1024]{2,1,0:T(8,128)(2,1)S(1)}, u32[]{:S(2)}, u32[]{:S(2)}) async-start(bf16[64,8,1024]{2,1,0:T(8,128)(2,1)} %shard_map.89), calls=%async_computation.1 | async-start | bytes 2097152 | tf_op jit(solution)/shard_map/all_to_all | solution.py:208
  64.1 0.0 copy-done.3
  64.1 0.1 shard_map.91
  64.2 3.4 %collective-permute-start.2 = (bf16[256,384]{1,0:T(8,128)(2,1)S(1)}, bf16[256,384]{1,0:T(8,128)(2,1)S(1)}, u32[]{:S(2)}, u32[]{:S(2)}) collective-permute-start(bf16[256,384]{1,0:T(8,128)(2,1)S(1)} %get-tuple-element.18), channel_id=1, source_target_pairs={{0,192},{192,384},{384,576},{576,0},{1,193},{193,385},{385,577},{5... | collective-permute-start | bytes 589832 | tf_op jit(solution)/shard_map/ppermute | solution.py:161
  67.6 3.0 %collective-permute-start.3 = (bf16[256,384]{1,0:T(8,128)(2,1)S(1)}, bf16[256,384]{1,0:T(8,128)(2,1)S(1)}, u32[]{:S(2)}, u32[]{:S(2)}) collective-permute-start(bf16[256,384]{1,0:T(8,128)(2,1)S(1)} %get-tuple-element.19), channel_id=1, source_target_pairs={{0,384},{192,576},{384,0},{576,192},{1,385},{193,577},{385,1},{577... | collective-permute-start | bytes 589832 | tf_op jit(solution)/shard_map/ppermute | solution.py:161
  70.6 4.1 %collective-permute-start.4 = (bf16[256,384]{1,0:T(8,128)(2,1)S(1)}, bf16[256,384]{1,0:T(8,128)(2,1)S(1)}, u32[]{:S(2)}, u32[]{:S(2)}) collective-permute-start(bf16[256,384]{1,0:T(8,128)(2,1)S(1)} %get-tuple-element.20), channel_id=1, source_target_pairs={{0,576},{192,0},{384,192},{576,384},{1,577},{193,1},{385,193},{577... | collective-permute-start | bytes 589832 | tf_op jit(solution)/shard_map/ppermute | solution.py:161
  74.7 0.0 collective-permute-done.2.refs_1_
  74.7 4.1 %collective-permute-done.3.refs_2_ = bf16[256,384]{1,0:T(8,128)(2,1)S(1)} collective-permute-done((bf16[256,384]{1,0:T(8,128)(2,1)S(1)}, bf16[256,384]{1,0:T(8,128)(2,1)S(1)}, u32[]{:S(2)}, u32[]{:S(2)}) %collective-permute-start.3) | collective-permute-done | bytes 196640 | tf_op jit(solution)/shard_map/ppermute | solution.py:161
  78.8 3.1 %collective-permute-done.4.refs_3_ = bf16[256,384]{1,0:T(8,128)(2,1)S(1)} collective-permute-done((bf16[256,384]{1,0:T(8,128)(2,1)S(1)}, bf16[256,384]{1,0:T(8,128)(2,1)S(1)}, u32[]{:S(2)}, u32[]{:S(2)}) %collective-permute-start.4) | collective-permute-done | bytes 196640 | tf_op jit(solution)/shard_map/ppermute | solution.py:161
  81.9 0.2 shard_map.92
  82.0 10.6 %collective-permute-start.5 = (bf16[256,128]{1,0:T(8,128)(2,1)S(1)}, bf16[256,128]{1,0:T(8,128)(2,1)S(1)}, u32[]{:S(2)}, u32[]{:S(2)}) collective-permute-start(bf16[256,128]{1,0:T(8,128)(2,1)S(1)} %get-tuple-element.22), channel_id=1, source_target_pairs={{0,64},{64,128},{128,0},{1,65},{65,129},{129,1},{2,66},{66,130},{1... | collective-permute-start | bytes 196616 | tf_op jit(solution)/shard_map/ppermute | solution.py:161
  92.7 3.2 %collective-permute-start.6 = (bf16[256,128]{1,0:T(8,128)(2,1)S(1)}, bf16[256,128]{1,0:T(8,128)(2,1)S(1)}, u32[]{:S(2)}, u32[]{:S(2)}) collective-permute-start(bf16[256,128]{1,0:T(8,128)(2,1)S(1)} %get-tuple-element.23), channel_id=1, source_target_pairs={{0,128},{64,0},{128,64},{1,129},{65,1},{129,65},{2,130},{66,2},{13... | collective-permute-start | bytes 196616 | tf_op jit(solution)/shard_map/ppermute | solution.py:161
  95.8 0.5 collective-permute-done.5.refs_1_
  96.3 8.7 %collective-permute-done.6.refs_2_ = bf16[256,128]{1,0:T(8,128)(2,1)S(1)} collective-permute-done((bf16[256,128]{1,0:T(8,128)(2,1)S(1)}, bf16[256,128]{1,0:T(8,128)(2,1)S(1)}, u32[]{:S(2)}, u32[]{:S(2)}) %collective-permute-start.6) | collective-permute-done | bytes 65568 | tf_op jit(solution)/shard_map/ppermute | solution.py:161
  105.0 0.7 shard_map.93
  105.6 0.0 all-to-all-done.1.in_ref
  105.7 0.0 copy-done.5
  105.7 0.0 copy-done.6
  105.7 0.8 shard_map.90
Async XLA Ops:
  0.6 45.5 %copy-start = (bf16[4096,224]{0,1:T(8,128)(2,1)S(1)}, bf16[4096,224]{0,1:T(8,128)(2,1)}, u32[]{:S(2)}) copy-start(bf16[4096,224]{0,1:T(8,128)(2,1)} %param.9) | copy-start | bytes 5505028
  1.5 0.8 copy-start.4
  44.2 4.7 %collective-permute-start = (bf16[64,8,1024]{2,1,0:T(8,128)(2,1)S(1)}, bf16[64,8,1024]{2,1,0:T(8,128)(2,1)}, u32[]{:S(2)}, u32[]{:S(2)}) collective-permute-start(bf16[64,8,1024]{2,1,0:T(8,128)(2,1)S(1)} %all_to_all.10.x_ref), channel_id=1, source_target_pairs={{0,1},{1,0},{2,3},{3,2},{4,5},{5,4},{6,7},{7,6},{8,9},{9,8},{10,11... | collective-permute-start | bytes 3145736 | tf_op jit(solution)/shard_map/ppermute | solution.py:161
  46.2 1.5 %copy-start.1 = (bf16[4096,224]{0,1:T(8,128)(2,1)S(1)}, bf16[4096,224]{0,1:T(8,128)(2,1)}, u32[]{:S(2)}) copy-start(bf16[4096,224]{0,1:T(8,128)(2,1)} %param.10) | copy-start | bytes 5505028
  47.7 1.5 %copy-start.2 = (bf16[224,4096]{1,0:T(8,128)(2,1)S(1)}, bf16[224,4096]{1,0:T(8,128)(2,1)}, u32[]{:S(2)}) copy-start(bf16[224,4096]{1,0:T(8,128)(2,1)} %down_ref.3) | copy-start | bytes 5505028
  51.6 4.7 %collective-permute-start.1 = (bf16[256,2048]{1,0:T(8,128)(2,1)S(1)}, bf16[256,2048]{1,0:T(8,128)(2,1)S(1)}, u32[]{:S(2)}, u32[]{:S(2)}) collective-permute-start(bf16[256,2048]{1,0:T(8,128)(2,1)S(1)} %get-tuple-element.16), channel_id=1, source_target_pairs={{0,1},{1,0},{2,3},{3,2},{4,5},{5,4},{6,7},{7,6},{8,9},{9,8},{10,11... | collective-permute-start | bytes 3145736 | tf_op jit(solution)/shard_map/ppermute | solution.py:161
  57.8 6.4 %copy-start.3 = (bf16[1,256,1536]{2,1,0:T(8,128)(2,1)S(1)}, bf16[1,256,1536]{2,1,0:T(8,128)(2,1)}, u32[]{:S(2)}) copy-start(bf16[1,256,1536]{2,1,0:T(8,128)(2,1)} %param.13) | copy-start | bytes 2359300
  57.8 47.9 %copy-start.5 = (bf16[4,4096]{1,0:T(4,128)(2,1)S(1)}, bf16[4,4096]{1,0:T(4,128)(2,1)}, u32[]{:S(2)}) copy-start(bf16[4,4096]{1,0:T(4,128)(2,1)} %tok_ref.3) | copy-start | bytes 98308
  57.8 47.9 %copy-start.6 = (s32[4,4096]{1,0:T(4,128)S(1)}, s32[4,4096]{1,0:T(4,128)}, u32[]{:S(2)}) copy-start(s32[4,4096]{1,0:T(4,128)} %mask_ref.1) | copy-start | bytes 196612
  57.8 47.9 %all-to-all-start.1 = ((bf16[64,8,1024]{2,1,0:T(8,128)(2,1)}), bf16[64,8,1024]{2,1,0:T(8,128)(2,1)S(1)}, u32[]{:S(2)}, u32[]{:S(2)}) async-start(bf16[64,8,1024]{2,1,0:T(8,128)(2,1)} %shard_map.89), calls=%async_computation.1 | async-start | bytes 2097152 | tf_op jit(solution)/shard_map/all_to_all | solution.py:208
  64.2 10.5 %collective-permute-start.2 = (bf16[256,384]{1,0:T(8,128)(2,1)S(1)}, bf16[256,384]{1,0:T(8,128)(2,1)S(1)}, u32[]{:S(2)}, u32[]{:S(2)}) collective-permute-start(bf16[256,384]{1,0:T(8,128)(2,1)S(1)} %get-tuple-element.18), channel_id=1, source_target_pairs={{0,192},{192,384},{384,576},{576,0},{1,193},{193,385},{385,577},{5... | collective-permute-start | bytes 589832 | tf_op jit(solution)/shard_map/ppermute | solution.py:161
  67.6 11.2 %collective-permute-start.3 = (bf16[256,384]{1,0:T(8,128)(2,1)S(1)}, bf16[256,384]{1,0:T(8,128)(2,1)S(1)}, u32[]{:S(2)}, u32[]{:S(2)}) collective-permute-start(bf16[256,384]{1,0:T(8,128)(2,1)S(1)} %get-tuple-element.19), channel_id=1, source_target_pairs={{0,384},{192,576},{384,0},{576,192},{1,385},{193,577},{385,1},{577... | collective-permute-start | bytes 589832 | tf_op jit(solution)/shard_map/ppermute | solution.py:161
  70.6 11.3 %collective-permute-start.4 = (bf16[256,384]{1,0:T(8,128)(2,1)S(1)}, bf16[256,384]{1,0:T(8,128)(2,1)S(1)}, u32[]{:S(2)}, u32[]{:S(2)}) collective-permute-start(bf16[256,384]{1,0:T(8,128)(2,1)S(1)} %get-tuple-element.20), channel_id=1, source_target_pairs={{0,576},{192,0},{384,192},{576,384},{1,577},{193,1},{385,193},{577... | collective-permute-start | bytes 589832 | tf_op jit(solution)/shard_map/ppermute | solution.py:161
  82.0 14.3 %collective-permute-start.5 = (bf16[256,128]{1,0:T(8,128)(2,1)S(1)}, bf16[256,128]{1,0:T(8,128)(2,1)S(1)}, u32[]{:S(2)}, u32[]{:S(2)}) collective-permute-start(bf16[256,128]{1,0:T(8,128)(2,1)S(1)} %get-tuple-element.22), channel_id=1, source_target_pairs={{0,64},{64,128},{128,0},{1,65},{65,129},{129,1},{2,66},{66,130},{1... | collective-permute-start | bytes 196616 | tf_op jit(solution)/shard_map/ppermute | solution.py:161
  92.7 12.3 %collective-permute-start.6 = (bf16[256,128]{1,0:T(8,128)(2,1)S(1)}, bf16[256,128]{1,0:T(8,128)(2,1)S(1)}, u32[]{:S(2)}, u32[]{:S(2)}) collective-permute-start(bf16[256,128]{1,0:T(8,128)(2,1)S(1)} %get-tuple-element.23), channel_id=1, source_target_pairs={{0,128},{64,0},{128,64},{1,129},{65,1},{129,65},{2,130},{66,2},{13... | collective-permute-start | bytes 196616 | tf_op jit(solution)/shard_map/ppermute | solution.py:161

commit v2 on v1

v2 whole, which is shorter than its diff:
```python
import functools

import jax
import jax.numpy as jnp
from jax import lax
from jax.experimental import pallas as pl
from jax.experimental.pallas import tpu as pltpu
from jax.sharding import Mesh
from jax.sharding import PartitionSpec as P

DP = ("x", "zh")
CHIPS = ("y", "zl")
TENSOR = CHIPS + ("c",)
BF16, F32 = jnp.bfloat16, jnp.float32
EPS = 1e-05
KEEP = 0.9


def call(body, outs, *args, smem=0, hbm=0, scratch=(), vmem=16, flops=0, moved=1 << 20):
    whole = pl.BlockSpec(memory_space=pltpu.VMEM)
    specs = [pl.BlockSpec(memory_space=pltpu.SMEM)] * smem
    specs += [whole] * (len(args) - smem - hbm)
    specs += [pl.BlockSpec(memory_space=pltpu.HBM)] * hbm
    return pl.pallas_call(
        body,
        out_shape=outs,
        in_specs=specs,
        out_specs=jax.tree.map(lambda _: whole, outs),
        scratch_shapes=list(scratch),
        compiler_params=pltpu.CompilerParams(vmem_limit_bytes=vmem << 20),
        cost_estimate=pl.CostEstimate(flops=flops, bytes_accessed=moved, transcendentals=0),
    )(*args)


def brought(pairs, sems):
    copies = [pltpu.make_async_copy(a, b, sems.at[i]) for i, (a, b) in enumerate(pairs)]
    for copy in copies:
        copy.start()
    return copies


def norm_body(tok_hbm, gain_hbm, out_ref, tok_ref, gain_ref, sems):
    half = tok_ref.shape[1] // 2
    for copy in brought(((tok_hbm, tok_ref), (gain_hbm, gain_ref)), sems):
        copy.wait()
    inputs = tok_ref[...].astype(F32)
    scale = lax.rsqrt(jnp.mean(inputs * inputs, axis=-1, keepdims=True) + EPS)
    normed = inputs * scale * gain_ref[...].astype(F32)[None, :]
    block = jnp.concatenate([normed[:, :half], normed[:, half:]], axis=0).astype(BF16)
    for i in range(out_ref.shape[0]):
        out_ref[i] = block


def paired(first, second):
    upper = lax.broadcasted_iota(jnp.int32, first.shape, 1) < first.shape[1] // 2
    turn = first.shape[1] // 2
    return (
        jnp.where(upper, first, pltpu.roll(second, turn, 1)),
        jnp.where(upper, pltpu.roll(first, turn, 1), second),
    )


def dot_t(x, w):
    return lax.dot_general(x, w, (((1,), (1,)), ((), ())), preferred_element_type=F32)


def ffn_body(x_ref, *refs):
    sent, out_ref, held, sems = refs[:6], refs[6], refs[7:13], refs[13]
    down_a, down_b = held[4:]
    copies = brought(list(zip(sent, held)), sems)
    blocks, eight, half = x_ref.shape
    rows = blocks * eight // 2
    x = x_ref[...].astype(F32).reshape(blocks // 2, 2, eight, half)
    left, right = (v.reshape(rows, half).astype(BF16) for v in paired(x[:, 0], x[:, 1]))

    def through(at):
        copies[at].wait()
        w_ref = held[at]
        return dot_t(left, w_ref[:, :half]) + dot_t(right, w_ref[:, half:])

    gates = [through(0), through(1)]
    ups = [through(2), through(3)]
    hidden = [(gate / (1.0 + jnp.exp(-gate)) * up).astype(BF16) for gate, up in zip(gates, ups)]
    copies[4].wait()
    copies[5].wait()
    step = min(half, 512)
    for k in range(half // step):
        sums = []
        for cols in (slice(k * step, (k + 1) * step), slice(half + k * step, half + (k + 1) * step)):
            part = jnp.dot(hidden[0], down_a[:, cols], preferred_element_type=F32)
            part += jnp.dot(hidden[1], down_b[:, cols], preferred_element_type=F32)
            sums.append(part.reshape(blocks // 2, eight, step))
        both = jnp.stack(paired(*sums), axis=1)
        out_ref[:, :, k * step : (k + 1) * step] = both.reshape(blocks, eight, step).astype(BF16)


def final_body(in_ref, tok_ref, mask_ref, out_ref):
    few, wide = tok_ref.shape
    half = wide // 2
    total = in_ref[0].astype(F32)
    for i in range(1, in_ref.shape[0]):
        total = total + in_ref[i].astype(F32)
    for q in range(2):
        cols = slice(q * half, (q + 1) * half)
        branch = total[q * few : (q + 1) * few]
        kept = mask_ref[:, cols].astype(F32) * branch / KEEP
        out_ref[:, cols] = (tok_ref[:, cols].astype(F32) + kept).astype(BF16)


def cut_body(place_ref, in_hbm, *refs):
    outs, sems = refs[:-1], refs[-1]
    width = outs[0].shape[1]
    pairs = []
    for k, out in enumerate(outs):
        at = lax.rem(place_ref[0] + k, len(outs)) * width
        pairs.append((in_hbm.at[:, pl.ds(pl.multiple_of(at, width), width)], out))
    for copy in brought(pairs, sems):
        copy.wait()


def sum_cut_body(place_ref, *refs, terms):
    total = refs[0][...].astype(F32)
    for ref in refs[1:terms]:
        total = total + ref[...].astype(F32)
    outs, held = refs[terms:-1], refs[-1]
    held[...] = total
    width = outs[0].shape[1]
    for k, out in enumerate(outs):
        at = lax.rem(place_ref[0] + k, len(outs)) * width
        out[...] = held[:, pl.ds(pl.multiple_of(at, width), width)].astype(out.dtype)


def sum_first_body(in_ref, out_ref):
    rows = 16
    for r in range(0, out_ref.shape[0], rows):
        total = in_ref[0, r : r + rows].astype(F32)
        for i in range(1, in_ref.shape[0]):
            total = total + in_ref[i, r : r + rows].astype(F32)
        out_ref[r : r + rows] = total.astype(BF16)


def sum_body(*refs):
    total = refs[0][...].astype(F32)
    for ref in refs[1:-1]:
        total = total + ref[...].astype(F32)
    refs[-1][...] = total


def shape(*dims, dtype=BF16):
    return jax.ShapeDtypeStruct(dims, dtype)


def place(axis):
    return lax.axis_index(axis).astype(jnp.int32).reshape(1)


def passed_on(x, axis, by):
    size = lax.axis_size(axis)
    return lax.ppermute(x, axis, [(i, (i + by) % size) for i in range(size)])


def bucket_over_x(bucket):
    rows, cols = bucket.shape
    nx = lax.axis_size("x")
    cut = call(
        cut_body, (shape(rows, cols // nx),) * nx, place("x"), bucket,
        smem=1, hbm=1, vmem=60, scratch=[pltpu.SemaphoreType.DMA((nx,))],
    )
    return [cut[0]] + [passed_on(cut[k], "x", k) for k in range(1, nx)]


def bucket_cut(terms):
    rows, wide = terms[0].shape
    nh = lax.axis_size("zh")
    return call(
        functools.partial(sum_cut_body, terms=len(terms)),
        (shape(rows, wide // nh),) * nh,
        place("zh"), *terms,
        smem=1, scratch=[pltpu.VMEM((rows, wide), F32)],
    )


def per_device(tokens, norm_gain, gate_weight, up_weight, down_weight, drop_mask, grad_bucket):
    few, wide = tokens.shape
    chips = lax.axis_size(CHIPS)
    units = gate_weight.shape[1]
    blocks = shape(chips, 2 * few, wide // 2)

    gathered = call(
        norm_body, blocks, tokens, norm_gain,
        hbm=2, vmem=60,
        scratch=[
            pltpu.VMEM(tokens.shape, BF16),
            pltpu.VMEM(norm_gain.shape, BF16),
            pltpu.SemaphoreType.DMA((2,)),
        ],
    )
    gathered = lax.all_to_all(gathered, CHIPS, 0, 0, tiled=True)
    bucket = bucket_over_x(grad_bucket[0])
    down_weight, bucket[1] = lax.optimization_barrier((down_weight, bucket[1]))
    weights = []
    for mine in (gate_weight.T, up_weight.T, down_weight):
        weights += [mine, passed_on(mine, "c", 1)]
    cut = bucket_cut(bucket)
    gathered, cut = lax.optimization_barrier((gathered, cut))
    terms = call(
        ffn_body, blocks, gathered, *weights,
        hbm=6,
        scratch=[pltpu.VMEM((units, wide), BF16)] * 6 + [pltpu.SemaphoreType.DMA((6,))],
        vmem=48, flops=12 * chips * few * wide * units, moved=14 * wide * units,
    )
    bucket = [cut[0]] + [passed_on(cut[k], "zh", k) for k in range(1, len(cut))]
    ny, nz = (lax.axis_size(axis) for axis in CHIPS)
    terms = terms.reshape(ny, nz * 2 * few, wide // 2)
    terms = lax.all_to_all(terms, "y", 0, 0, tiled=True)
    terms = call(sum_first_body, shape(nz * 2 * few, wide // 2), terms)
    terms, bucket = lax.optimization_barrier((terms.reshape(nz, 2 * few, wide // 2), bucket))
    terms = lax.all_to_all(terms, "zl", 0, 0, tiled=True)
    reduced = call(sum_body, shape(*cut[0].shape, dtype=F32), *bucket)
    mixed = call(final_body, shape(few, wide), terms, tokens, drop_mask)
    return (mixed, reduced)


def solution(mesh):
    finer = Mesh(mesh.devices.reshape(4, 3, 8, 4, 2), DP + TENSOR)
    return jax.shard_map(
        per_device,
        mesh=finer,
        in_specs=(
            P(DP + TENSOR, None),
            P(),
            P(None, TENSOR),
            P(None, TENSOR),
            P(TENSOR, None),
            P(DP + TENSOR, None),
            P(DP, TENSOR, None),
        ),
        out_specs=(P(DP + TENSOR, None), P(TENSOR, DP)),
        check_vma=False,
    )
```

time: 107 us -> 101 us (0.944)
  the two profiles are of different devices: /device:TPU:10 before, /device:TPU:6 now
where the time goes in v2:
time: 101 us
  starting transfers between devices  53.1 us (53%)
  waiting for transfers between devices  31 us (31%)
  Pallas kernels  13.6 us (13%)
  local copies, waits for them, and re-layouts  2.19 us (2%)
    ppermute x8, starting transfers between devices, passed_on(): return lax.ppermute(x, axis, [(i, (i + by) % size) for i in range(size)])  28.8 us
    all_to_all x1, waiting for transfers between devices, per_device(): terms = lax.all_to_all(terms, 'y', 0, 0, tiled=True)  15.2 us
    pallas_call x7, Pallas kernels, call(): pl.pallas_call(body, out_shape=outs, in_specs=specs, out_specs=jax.tree.m...  13.6 us
    all_to_all x1, starting transfers between devices, per_device(): gathered = lax.all_to_all(gathered, CHIPS, 0, 0, tiled=True)  12.9 us
    ppermute x8, waiting for transfers between devices, passed_on(): return lax.ppermute(x, axis, [(i, (i + by) % size) for i in range(size)])  10.4 us
    all_to_all x1, starting transfers between devices, per_device(): terms = lax.all_to_all(terms, 'y', 0, 0, tiled=True)  6.85 us
    all_to_all x1, waiting for transfers between devices, per_device(): terms = lax.all_to_all(terms, 'zl', 0, 0, tiled=True)  5.41 us
    all_to_all x1, starting transfers between devices, per_device(): terms = lax.all_to_all(terms, 'zl', 0, 0, tiled=True)  4.53 us
  transfers between devices with their start and end apart: 11, of which 5 were waited for; matrix products, arithmetic and copies ran while one was open for 0% of the time, Pallas kernels for 4%

profile of v2, /device:TPU:6, one launch (start us, length us, event | category | flops | bytes accessed | tf_op | source)
XLA Modules:
  0.0 100.7 jit_solution(11488058310341037348)
XLA Ops:
  0.6 0.0 copy-start
  0.6 2.1 %shard_map.86 = bf16[32,8,2048]{2,1,0:T(8,128)(2,1)} custom-call(bf16[4,4096]{1,0:T(4,128)(2,1)} %tok_ref.1, bf16[4096]{0:T(1024)(128)(2,1)} %gain_hbm.1), custom_call_target="tpu_custom_call" | custom-call | bytes 1048576 | tf_op jit(solution)/shard_map/pallas_call | solution.py:24
  2.8 12.9 %all-to-all-start = ((bf16[32,8,2048]{2,1,0:T(8,128)(2,1)}), bf16[32,8,2048]{2,1,0:T(8,128)(2,1)S(1)}, u32[]{:S(2)}, u32[]{:S(2)}) async-start(bf16[32,8,2048]{2,1,0:T(8,128)(2,1)} %shard_map.86), calls=%async_computation | async-start | bytes 2097152 | tf_op jit(solution)/shard_map/all_to_all | solution.py:198
  15.7 2.2 %shard_map.87 = (bf16[256,384]{1,0:T(8,128)(2,1)}, bf16[256,384]{1,0:T(8,128)(2,1)}, bf16[256,384]{1,0:T(8,128)(2,1)}, bf16[256,384]{1,0:T(8,128)(2,1)}) custom-call(s32[1]{0:T(128)} %bitcast.1.place_ref, bf16[256,1536]{1,0:T(8,128)(2,1)} %bitcast.11), custom_call_target="tpu_custom_call" | custom-call | bytes 1048576 | tf_op jit(solution)/shard_map/pallas_call | solution.py:24
  17.9 2.4 %collective-permute-start = (bf16[256,384]{1,0:T(8,128)(2,1)}, bf16[256,384]{1,0:T(8,128)(2,1)S(1)}, u32[]{:S(2)}, u32[]{:S(2)}) collective-permute-start(bf16[256,384]{1,0:T(8,128)(2,1)} %get-tuple-element.20), channel_id=1, source_target_pairs={{0,192},{192,384},{384,576},{576,0},{1,193},{193,385},{385,577},{5... | collective-permute-start | bytes 589832 | tf_op jit(solution)/shard_map/ppermute | solution.py:159
  20.3 0.0 copy-done
  20.3 1.9 %collective-permute-start.3 = (bf16[224,4096]{1,0:T(8,128)(2,1)S(1)}, bf16[224,4096]{1,0:T(8,128)(2,1)}, u32[]{:S(2)}, u32[]{:S(2)}) collective-permute-start(bf16[224,4096]{1,0:T(8,128)(2,1)S(1)} %bitcast.7), channel_id=1, source_target_pairs={{0,1},{1,0},{2,3},{3,2},{4,5},{5,4},{6,7},{7,6},{8,9},{9,8},{10,11... | collective-permute-start | bytes 5505032 | tf_op jit(solution)/shard_map/ppermute | solution.py:159
  22.2 2.4 %collective-permute-start.4 = (bf16[224,4096]{1,0:T(8,128)(2,1)}, bf16[224,4096]{1,0:T(8,128)(2,1)}, u32[]{:S(2)}, u32[]{:S(2)}) collective-permute-start(bf16[224,4096]{1,0:T(8,128)(2,1)} %bitcast.9), channel_id=1, source_target_pairs={{0,1},{1,0},{2,3},{3,2},{4,5},{5,4},{6,7},{7,6},{8,9},{9,8},{10,11... | collective-permute-start | bytes 5505032 | tf_op jit(solution)/shard_map/ppermute | solution.py:159
  24.6 1.7 %collective-permute-done.refs_1_ = bf16[256,384]{1,0:T(8,128)(2,1)S(1)} collective-permute-done((bf16[256,384]{1,0:T(8,128)(2,1)}, bf16[256,384]{1,0:T(8,128)(2,1)S(1)}, u32[]{:S(2)}, u32[]{:S(2)}) %collective-permute-start) | collective-permute-done | bytes 196640 | tf_op jit(solution)/shard_map/ppermute | solution.py:159
  26.3 1.9 %collective-permute-start.5 = (bf16[224,4096]{1,0:T(8,128)(2,1)}, bf16[224,4096]{1,0:T(8,128)(2,1)}, u32[]{:S(2)}, u32[]{:S(2)}) collective-permute-start(bf16[224,4096]{1,0:T(8,128)(2,1)} %refs_4_), channel_id=1, source_target_pairs={{0,1},{1,0},{2,3},{3,2},{4,5},{5,4},{6,7},{7,6},{8,9},{9,8},{10,11... | collective-permute-start | bytes 5505032 | tf_op jit(solution)/shard_map/ppermute | solution.py:159
  28.3 3.3 %collective-permute-start.1 = (bf16[256,384]{1,0:T(8,128)(2,1)}, bf16[256,384]{1,0:T(8,128)(2,1)S(1)}, u32[]{:S(2)}, u32[]{:S(2)}) collective-permute-start(bf16[256,384]{1,0:T(8,128)(2,1)} %get-tuple-element.22), channel_id=1, source_target_pairs={{0,384},{192,576},{384,0},{576,192},{1,385},{193,577},{385,1},{577... | collective-permute-start | bytes 589832 | tf_op jit(solution)/shard_map/ppermute | solution.py:159
  31.6 3.0 %collective-permute-start.2 = (bf16[256,384]{1,0:T(8,128)(2,1)}, bf16[256,384]{1,0:T(8,128)(2,1)S(1)}, u32[]{:S(2)}, u32[]{:S(2)}) collective-permute-start(bf16[256,384]{1,0:T(8,128)(2,1)} %get-tuple-element.23), channel_id=1, source_target_pairs={{0,576},{192,0},{384,192},{576,384},{1,577},{193,1},{385,193},{577... | collective-permute-start | bytes 589832 | tf_op jit(solution)/shard_map/ppermute | solution.py:159
  34.6 4.9 %collective-permute-done.1.refs_2_ = bf16[256,384]{1,0:T(8,128)(2,1)S(1)} collective-permute-done((bf16[256,384]{1,0:T(8,128)(2,1)}, bf16[256,384]{1,0:T(8,128)(2,1)S(1)}, u32[]{:S(2)}, u32[]{:S(2)}) %collective-permute-start.1) | collective-permute-done | bytes 196640 | tf_op jit(solution)/shard_map/ppermute | solution.py:159
  39.6 3.8 %collective-permute-done.2.refs_3_ = bf16[256,384]{1,0:T(8,128)(2,1)S(1)} collective-permute-done((bf16[256,384]{1,0:T(8,128)(2,1)}, bf16[256,384]{1,0:T(8,128)(2,1)S(1)}, u32[]{:S(2)}, u32[]{:S(2)}) %collective-permute-start.2) | collective-permute-done | bytes 196640 | tf_op jit(solution)/shard_map/ppermute | solution.py:159
  43.4 0.0 copy-start.1
  43.4 0.9 copy-done.1
  44.3 0.2 shard_map.88
  44.5 0.0 copy-start.4
  44.5 0.6 copy-done.4
  45.1 0.0 copy-start.6
  45.1 0.6 copy-done.6
  45.7 0.0 all-to-all-done.x_ref
  45.7 0.0 collective-permute-done.3.refs_1_
  45.7 0.0 collective-permute-done.4.refs_3_
  45.7 0.0 collective-permute-done.5.refs_5_
  45.7 7.0 %shard_map.89 = bf16[32,8,2048]{2,1,0:T(8,128)(2,1)} custom-call(bf16[32,8,2048]{2,1,0:T(8,128)(2,1)S(1)} %all-to-all-done.x_ref, bf16[224,4096]{1,0:T(8,128)(2,1)S(1)} %bitcast.8, bf16[224,4096]{1,0:T(8,128)(2,1)} %collective-permute-done.3.refs_1_, bf16[224,4096]{1,0:T(8,128)(2,1)} %bitcast.10, bf16[224,4096]{1,0:T(8,128)(2,1)} %collective-permute-done.4.refs_3_, ...), custom_call_target="tpu_custom_call" | custom-call | flops 1409286144 | bytes 12845056 | tf_op jit(solution)/shard_map/pallas_call | solution.py:24
  52.8 0.0 copy-start.7
  52.8 0.0 copy-start.5
  52.8 0.0 copy-start.2
  52.8 0.0 copy-start.3
  52.8 6.8 %all-to-all-start.1 = ((bf16[8,32,2048]{2,1,0:T(8,128)(2,1)}), bf16[8,32,2048]{2,1,0:T(8,128)(2,1)S(1)}, u32[]{:S(2)}, u32[]{:S(2)}) async-start(bf16[8,32,2048]{2,1,0:T(8,128)(2,1)} %bitcast.5), calls=%async_computation.1 | async-start | bytes 2097152 | tf_op jit(solution)/shard_map/all_to_all | solution.py:215
  59.7 0.0 copy-done.7
  59.7 10.6 %collective-permute-start.6 = (bf16[256,128]{1,0:T(8,128)(2,1)S(1)}, bf16[256,128]{1,0:T(8,128)(2,1)S(1)}, u32[]{:S(2)}, u32[]{:S(2)}) collective-permute-start(bf16[256,128]{1,0:T(8,128)(2,1)S(1)} %copy-done.7), channel_id=1, source_target_pairs={{0,64},{64,128},{128,0},{1,65},{65,129},{129,1},{2,66},{66,130},{1... | collective-permute-start | bytes 196616 | tf_op jit(solution)/shard_map/ppermute | solution.py:159
  70.3 0.0 copy-done.5
  70.3 3.2 %collective-permute-start.7 = (bf16[256,128]{1,0:T(8,128)(2,1)S(1)}, bf16[256,128]{1,0:T(8,128)(2,1)S(1)}, u32[]{:S(2)}, u32[]{:S(2)}) collective-permute-start(bf16[256,128]{1,0:T(8,128)(2,1)S(1)} %copy-done.5), channel_id=1, source_target_pairs={{0,128},{64,0},{128,64},{1,129},{65,1},{129,65},{2,130},{66,2},{13... | collective-permute-start | bytes 196616 | tf_op jit(solution)/shard_map/ppermute | solution.py:159
  73.5 15.2 %all-to-all-done.1.in_ref = bf16[8,32,2048]{2,1,0:T(8,128)(2,1)S(1)} async-done(((bf16[8,32,2048]{2,1,0:T(8,128)(2,1)}), bf16[8,32,2048]{2,1,0:T(8,128)(2,1)S(1)}, u32[]{:S(2)}, u32[]{:S(2)}) %all-to-all-start.1) | async-done | bytes 1048608 | tf_op jit(solution)/shard_map/all_to_all | solution.py:215
  88.6 0.8 shard_map.90
  89.4 0.0 collective-permute-done.6.refs_1_
  89.4 0.0 collective-permute-done.7.refs_2_
  89.4 4.5 %all-to-all-start.2 = ((bf16[4,8,2048]{2,1,0:T(8,128)(2,1)}), bf16[4,8,2048]{2,1,0:T(8,128)(2,1)S(1)}, u32[]{:S(2)}, u32[]{:S(2)}) async-start(bf16[4,8,2048]{2,1,0:T(8,128)(2,1)} %bitcast.6), calls=%async_computation.2 | async-start | bytes 262144 | tf_op jit(solution)/shard_map/all_to_all | solution.py:218
  94.0 0.7 shard_map.92
  94.6 5.4 %all-to-all-done.2.in_ref = bf16[4,8,2048]{2,1,0:T(8,128)(2,1)S(1)} async-done(((bf16[4,8,2048]{2,1,0:T(8,128)(2,1)}), bf16[4,8,2048]{2,1,0:T(8,128)(2,1)S(1)}, u32[]{:S(2)}, u32[]{:S(2)}) %all-to-all-start.2) | async-done | bytes 131104 | tf_op jit(solution)/shard_map/all_to_all | solution.py:218
  100.1 0.0 copy-done.2
  100.1 0.0 copy-done.3
  100.1 0.7 shard_map.91
Async XLA Ops:
  0.6 19.7 %copy-start = (bf16[4096,224]{0,1:T(8,128)(2,1)S(1)}, bf16[4096,224]{0,1:T(8,128)(2,1)}, u32[]{:S(2)}) copy-start(bf16[4096,224]{0,1:T(8,128)(2,1)} %param.9) | copy-start | bytes 5505028
  2.8 43.0 %all-to-all-start = ((bf16[32,8,2048]{2,1,0:T(8,128)(2,1)}), bf16[32,8,2048]{2,1,0:T(8,128)(2,1)S(1)}, u32[]{:S(2)}, u32[]{:S(2)}) async-start(bf16[32,8,2048]{2,1,0:T(8,128)(2,1)} %shard_map.86), calls=%async_computation | async-start | bytes 2097152 | tf_op jit(solution)/shard_map/all_to_all | solution.py:198
  17.9 8.5 %collective-permute-start = (bf16[256,384]{1,0:T(8,128)(2,1)}, bf16[256,384]{1,0:T(8,128)(2,1)S(1)}, u32[]{:S(2)}, u32[]{:S(2)}) collective-permute-start(bf16[256,384]{1,0:T(8,128)(2,1)} %get-tuple-element.20), channel_id=1, source_target_pairs={{0,192},{192,384},{384,576},{576,0},{1,193},{193,385},{385,577},{5... | collective-permute-start | bytes 589832 | tf_op jit(solution)/shard_map/ppermute | solution.py:159
  20.3 25.4 %collective-permute-start.3 = (bf16[224,4096]{1,0:T(8,128)(2,1)S(1)}, bf16[224,4096]{1,0:T(8,128)(2,1)}, u32[]{:S(2)}, u32[]{:S(2)}) collective-permute-start(bf16[224,4096]{1,0:T(8,128)(2,1)S(1)} %bitcast.7), channel_id=1, source_target_pairs={{0,1},{1,0},{2,3},{3,2},{4,5},{5,4},{6,7},{7,6},{8,9},{9,8},{10,11... | collective-permute-start | bytes 5505032 | tf_op jit(solution)/shard_map/ppermute | solution.py:159
  22.2 23.5 %collective-permute-start.4 = (bf16[224,4096]{1,0:T(8,128)(2,1)}, bf16[224,4096]{1,0:T(8,128)(2,1)}, u32[]{:S(2)}, u32[]{:S(2)}) collective-permute-start(bf16[224,4096]{1,0:T(8,128)(2,1)} %bitcast.9), channel_id=1, source_target_pairs={{0,1},{1,0},{2,3},{3,2},{4,5},{5,4},{6,7},{7,6},{8,9},{9,8},{10,11... | collective-permute-start | bytes 5505032 | tf_op jit(solution)/shard_map/ppermute | solution.py:159
  26.3 19.4 %collective-permute-start.5 = (bf16[224,4096]{1,0:T(8,128)(2,1)}, bf16[224,4096]{1,0:T(8,128)(2,1)}, u32[]{:S(2)}, u32[]{:S(2)}) collective-permute-start(bf16[224,4096]{1,0:T(8,128)(2,1)} %refs_4_), channel_id=1, source_target_pairs={{0,1},{1,0},{2,3},{3,2},{4,5},{5,4},{6,7},{7,6},{8,9},{9,8},{10,11... | collective-permute-start | bytes 5505032 | tf_op jit(solution)/shard_map/ppermute | solution.py:159
  28.3 11.3 %collective-permute-start.1 = (bf16[256,384]{1,0:T(8,128)(2,1)}, bf16[256,384]{1,0:T(8,128)(2,1)S(1)}, u32[]{:S(2)}, u32[]{:S(2)}) collective-permute-start(bf16[256,384]{1,0:T(8,128)(2,1)} %get-tuple-element.22), channel_id=1, source_target_pairs={{0,384},{192,576},{384,0},{576,192},{1,385},{193,577},{385,1},{577... | collective-permute-start | bytes 589832 | tf_op jit(solution)/shard_map/ppermute | solution.py:159
  31.6 11.8 %collective-permute-start.2 = (bf16[256,384]{1,0:T(8,128)(2,1)}, bf16[256,384]{1,0:T(8,128)(2,1)S(1)}, u32[]{:S(2)}, u32[]{:S(2)}) collective-permute-start(bf16[256,384]{1,0:T(8,128)(2,1)} %get-tuple-element.23), channel_id=1, source_target_pairs={{0,576},{192,0},{384,192},{576,384},{1,577},{193,1},{385,193},{577... | collective-permute-start | bytes 589832 | tf_op jit(solution)/shard_map/ppermute | solution.py:159
  43.4 0.9 copy-start.1
  44.5 0.6 copy-start.4
  45.1 0.6 copy-start.6
  52.8 6.9 %copy-start.7 = (bf16[256,128]{1,0:T(8,128)(2,1)S(1)}, bf16[256,128]{1,0:T(8,128)(2,1)}, u32[]{:S(2)}) copy-start(bf16[256,128]{1,0:T(8,128)(2,1)} %copy-done.6) | copy-start | bytes 196612
  52.8 17.5 %copy-start.5 = (bf16[256,128]{1,0:T(8,128)(2,1)S(1)}, bf16[256,128]{1,0:T(8,128)(2,1)}, u32[]{:S(2)}) copy-start(bf16[256,128]{1,0:T(8,128)(2,1)} %copy-done.4) | copy-start | bytes 196612
  52.8 47.3 %copy-start.2 = (bf16[4,4096]{1,0:T(4,128)(2,1)S(1)}, bf16[4,4096]{1,0:T(4,128)(2,1)}, u32[]{:S(2)}) copy-start(bf16[4,4096]{1,0:T(4,128)(2,1)} %tok_ref.1) | copy-start | bytes 98308
  52.8 47.3 %copy-start.3 = (s32[4,4096]{1,0:T(4,128)S(1)}, s32[4,4096]{1,0:T(4,128)}, u32[]{:S(2)}) copy-start(s32[4,4096]{1,0:T(4,128)} %mask_ref.1) | copy-start | bytes 196612
  52.8 35.8 %all-to-all-start.1 = ((bf16[8,32,2048]{2,1,0:T(8,128)(2,1)}), bf16[8,32,2048]{2,1,0:T(8,128)(2,1)S(1)}, u32[]{:S(2)}, u32[]{:S(2)}) async-start(bf16[8,32,2048]{2,1,0:T(8,128)(2,1)} %bitcast.5), calls=%async_computation.1 | async-start | bytes 2097152 | tf_op jit(solution)/shard_map/all_to_all | solution.py:215
  59.7 29.8 %collective-permute-start.6 = (bf16[256,128]{1,0:T(8,128)(2,1)S(1)}, bf16[256,128]{1,0:T(8,128)(2,1)S(1)}, u32[]{:S(2)}, u32[]{:S(2)}) collective-permute-start(bf16[256,128]{1,0:T(8,128)(2,1)S(1)} %copy-done.7), channel_id=1, source_target_pairs={{0,64},{64,128},{128,0},{1,65},{65,129},{129,1},{2,66},{66,130},{1... | collective-permute-start | bytes 196616 | tf_op jit(solution)/shard_map/ppermute | solution.py:159
  70.3 19.1 %collective-permute-start.7 = (bf16[256,128]{1,0:T(8,128)(2,1)S(1)}, bf16[256,128]{1,0:T(8,128)(2,1)S(1)}, u32[]{:S(2)}, u32[]{:S(2)}) collective-permute-start(bf16[256,128]{1,0:T(8,128)(2,1)S(1)} %copy-done.5), channel_id=1, source_target_pairs={{0,128},{64,0},{128,64},{1,129},{65,1},{129,65},{2,130},{66,2},{13... | collective-permute-start | bytes 196616 | tf_op jit(solution)/shard_map/ppermute | solution.py:159
  89.4 10.6 %all-to-all-start.2 = ((bf16[4,8,2048]{2,1,0:T(8,128)(2,1)}), bf16[4,8,2048]{2,1,0:T(8,128)(2,1)S(1)}, u32[]{:S(2)}, u32[]{:S(2)}) async-start(bf16[4,8,2048]{2,1,0:T(8,128)(2,1)} %bitcast.6), calls=%async_computation.2 | async-start | bytes 262144 | tf_op jit(solution)/shard_map/all_to_all | solution.py:218

commit v3 on v2

--- a/solution.py
+++ b/solution.py
@@ -118,32 +118,21 @@
         copy.wait()
 
 
-def sum_cut_body(place_ref, *refs, terms):
-    total = refs[0][...].astype(F32)
-    for ref in refs[1:terms]:
-        total = total + ref[...].astype(F32)
-    outs, held = refs[terms:-1], refs[-1]
-    held[...] = total
-    width = outs[0].shape[1]
-    for k, out in enumerate(outs):
-        at = lax.rem(place_ref[0] + k, len(outs)) * width
-        out[...] = held[:, pl.ds(pl.multiple_of(at, width), width)].astype(out.dtype)
-
-
-def sum_first_body(in_ref, out_ref):
-    rows = 16
-    for r in range(0, out_ref.shape[0], rows):
-        total = in_ref[0, r : r + rows].astype(F32)
-        for i in range(1, in_ref.shape[0]):
-            total = total + in_ref[i, r : r + rows].astype(F32)
-        out_ref[r : r + rows] = total.astype(BF16)
-
-
-def sum_body(*refs):
+def sum_cut_body(*refs):
     total = refs[0][...].astype(F32)
     for ref in refs[1:-1]:
         total = total + ref[...].astype(F32)
-    refs[-1][...] = total
+    out_ref = refs[-1]
+    width = out_ref.shape[-1]
+    for k in range(out_ref.shape[0]):
+        out_ref[k] = total[:, k * width : (k + 1) * width].astype(BF16)
+
+
+def sum_parts_body(in_ref, out_ref):
+    total = in_ref[0].astype(F32)
+    for k in range(1, in_ref.shape[0]):
+        total = total + in_ref[k].astype(F32)
+    out_ref[...] = total
 
 
 def shape(*dims, dtype=BF16):
@@ -172,12 +161,7 @@
 def bucket_cut(terms):
     rows, wide = terms[0].shape
     nh = lax.axis_size("zh")
-    return call(
-        functools.partial(sum_cut_body, terms=len(terms)),
-        (shape(rows, wide // nh),) * nh,
-        place("zh"), *terms,
-        smem=1, scratch=[pltpu.VMEM((rows, wide), F32)],
-    )
+    return call(sum_cut_body, shape(nh, rows, wide // nh), *terms)
 
 
 def per_device(tokens, norm_gain, gate_weight, up_weight, down_weight, drop_mask, grad_bucket):
@@ -203,20 +187,16 @@
         weights += [mine, passed_on(mine, "c", 1)]
     cut = bucket_cut(bucket)
     gathered, cut = lax.optimization_barrier((gathered, cut))
+    bucket = lax.all_to_all(cut, "zh", 0, 0, tiled=True)
     terms = call(
         ffn_body, blocks, gathered, *weights,
         hbm=6,
         scratch=[pltpu.VMEM((units, wide), BF16)] * 6 + [pltpu.SemaphoreType.DMA((6,))],
         vmem=48, flops=12 * chips * few * wide * units, moved=14 * wide * units,
     )
-    bucket = [cut[0]] + [passed_on(cut[k], "zh", k) for k in range(1, len(cut))]
-    ny, nz = (lax.axis_size(axis) for axis in CHIPS)
-    terms = terms.reshape(ny, nz * 2 * few, wide // 2)
-    terms = lax.all_to_all(terms, "y", 0, 0, tiled=True)
-    terms = call(sum_first_body, shape(nz * 2 * few, wide // 2), terms)
-    terms, bucket = lax.optimization_barrier((terms.reshape(nz, 2 * few, wide // 2), bucket))
-    terms = lax.all_to_all(terms, "zl", 0, 0, tiled=True)
-    reduced = call(sum_body, shape(*cut[0].shape, dtype=F32), *bucket)
+    terms, bucket = lax.optimization_barrier((terms, bucket))
+    terms = lax.all_to_all(terms, CHIPS, 0, 0, tiled=True)
+    reduced = call(sum_parts_body, shape(*cut.shape[1:], dtype=F32), bucket)
     mixed = call(final_body, shape(few, wide), terms, tokens, drop_mask)
     return (mixed, reduced)
 

time: 101 us -> 108 us (1.069); the launches traced: 101 us -> 107 us
  waiting for transfers between devices: 31 us -> 39.8 us
  starting transfers between devices: 53.1 us -> 51.5 us
  local copies, waits for them, and re-layouts: 2.19 us -> 0.94 us
    ppermute x8 -> x6, starting transfers between devices: 28.8 us -> 15 us  [passed_on(): return lax.ppermute(x, axis, [(i, (i + by) % size) for i in range(size)])]
    all_to_all x2, starting transfers between devices: 11.4 us -> 23.5 us  [the longest x1 12.3 us: per_device(): terms = lax.all_to_all(terms, CHIPS, 0, 0, tiled=True)]
    all_to_all x2, waiting for transfers between devices: 20.6 us -> 29.4 us  [the longest x1 26.8 us: per_device(): terms = lax.all_to_all(terms, CHIPS, 0, 0, tiled=True)]
    unnamed x16 -> x8, local copies, waits for them, and re-layouts: 2.19 us -> 0.94 us
    pallas_call x7 -> x6, Pallas kernels: 13.6 us -> 13.5 us  [call(): pl.pallas_call(body, out_shape=outs, in_specs=specs, out_specs=jax.tree.m...]
    ppermute x8 -> x6, waiting for transfers between devices: 10.4 us -> 10.4 us  [passed_on(): return lax.ppermute(x, axis, [(i, (i + by) % size) for i in range(size)])]
  transfers between devices with their start and end apart: 11 -> 9, of which waited for: 5 -> 5; matrix products, arithmetic and copies ran while one was open for 0% -> 0% of each run, Pallas kernels for 4% -> 10%
where the time goes in v3:
time: 108 us; the launch traced here: 107 us
  starting transfers between devices  51.5 us (48%)
  waiting for transfers between devices  39.8 us (37%)
  Pallas kernels  13.5 us (12%)
    all_to_all x1, waiting for transfers between devices, per_device(): terms = lax.all_to_all(terms, CHIPS, 0, 0, tiled=True)  26.8 us
    ppermute x6, starting transfers between devices, passed_on(): return lax.ppermute(x, axis, [(i, (i + by) % size) for i in range(size)])  15 us
    pallas_call x6, Pallas kernels, call(): pl.pallas_call(body, out_shape=outs, in_specs=specs, out_specs=jax.tree.m...  13.5 us
    all_to_all x1, starting transfers between devices, per_device(): gathered = lax.all_to_all(gathered, CHIPS, 0, 0, tiled=True)  12.9 us
    all_to_all x1, starting transfers between devices, per_device(): terms = lax.all_to_all(terms, CHIPS, 0, 0, tiled=True)  12.3 us
    all_to_all x1, starting transfers between devices, per_device(): bucket = lax.all_to_all(cut, 'zh', 0, 0, tiled=True)  11.2 us
    ppermute x6, waiting for transfers between devices, passed_on(): return lax.ppermute(x, axis, [(i, (i + by) % size) for i in range(size)])  10.4 us
    all_to_all x1, waiting for transfers between devices, per_device(): bucket = lax.all_to_all(cut, 'zh', 0, 0, tiled=True)  2.55 us
  transfers between devices with their start and end apart: 9, of which 5 were waited for; matrix products, arithmetic and copies ran while one was open for 0% of the time, Pallas kernels for 10%

profile of v3, /device:TPU:6, one launch (start us, length us, event | category | flops | bytes accessed | tf_op | source)
XLA Modules:
  0.0 106.5 jit_solution(2980862903801816070)
XLA Ops:
  0.6 0.0 copy-start
  0.6 2.1 %shard_map.86 = bf16[32,8,2048]{2,1,0:T(8,128)(2,1)} custom-call(bf16[4,4096]{1,0:T(4,128)(2,1)} %tok_ref.1, bf16[4096]{0:T(1024)(128)(2,1)} %gain_hbm.1), custom_call_target="tpu_custom_call" | custom-call | bytes 1048576 | tf_op jit(solution)/shard_map/pallas_call | solution.py:24
  2.7 12.9 %all-to-all-start = ((bf16[32,8,2048]{2,1,0:T(8,128)(2,1)}), bf16[32,8,2048]{2,1,0:T(8,128)(2,1)S(1)}, u32[]{:S(2)}, u32[]{:S(2)}) async-start(bf16[32,8,2048]{2,1,0:T(8,128)(2,1)} %shard_map.86), calls=%async_computation | async-start | bytes 2097152 | tf_op jit(solution)/shard_map/all_to_all | solution.py:182
  15.7 2.2 %shard_map.87 = (bf16[256,384]{1,0:T(8,128)(2,1)}, bf16[256,384]{1,0:T(8,128)(2,1)}, bf16[256,384]{1,0:T(8,128)(2,1)}, bf16[256,384]{1,0:T(8,128)(2,1)}) custom-call(s32[1]{0:T(128)} %bitcast.place_ref, bf16[256,1536]{1,0:T(8,128)(2,1)} %bitcast.8), custom_call_target="tpu_custom_call" | custom-call | bytes 1048576 | tf_op jit(solution)/shard_map/pallas_call | solution.py:24
  17.9 2.4 %collective-permute-start = (bf16[256,384]{1,0:T(8,128)(2,1)}, bf16[256,384]{1,0:T(8,128)(2,1)S(1)}, u32[]{:S(2)}, u32[]{:S(2)}) collective-permute-start(bf16[256,384]{1,0:T(8,128)(2,1)} %get-tuple-element.13), channel_id=1, source_target_pairs={{0,192},{192,384},{384,576},{576,0},{1,193},{193,385},{385,577},{5... | collective-permute-start | bytes 589832 | tf_op jit(solution)/shard_map/ppermute | solution.py:148
  20.3 0.0 copy-done
  20.3 1.9 %collective-permute-start.3 = (bf16[224,4096]{1,0:T(8,128)(2,1)S(1)}, bf16[224,4096]{1,0:T(8,128)(2,1)}, u32[]{:S(2)}, u32[]{:S(2)}) collective-permute-start(bf16[224,4096]{1,0:T(8,128)(2,1)S(1)} %bitcast.4), channel_id=1, source_target_pairs={{0,1},{1,0},{2,3},{3,2},{4,5},{5,4},{6,7},{7,6},{8,9},{9,8},{10,11... | collective-permute-start | bytes 5505032 | tf_op jit(solution)/shard_map/ppermute | solution.py:148
  22.2 2.4 %collective-permute-start.4 = (bf16[224,4096]{1,0:T(8,128)(2,1)}, bf16[224,4096]{1,0:T(8,128)(2,1)}, u32[]{:S(2)}, u32[]{:S(2)}) collective-permute-start(bf16[224,4096]{1,0:T(8,128)(2,1)} %bitcast.6), channel_id=1, source_target_pairs={{0,1},{1,0},{2,3},{3,2},{4,5},{5,4},{6,7},{7,6},{8,9},{9,8},{10,11... | collective-permute-start | bytes 5505032 | tf_op jit(solution)/shard_map/ppermute | solution.py:148
  24.7 1.7 %collective-permute-done.refs_1_ = bf16[256,384]{1,0:T(8,128)(2,1)S(1)} collective-permute-done((bf16[256,384]{1,0:T(8,128)(2,1)}, bf16[256,384]{1,0:T(8,128)(2,1)S(1)}, u32[]{:S(2)}, u32[]{:S(2)}) %collective-permute-start) | collective-permute-done | bytes 196640 | tf_op jit(solution)/shard_map/ppermute | solution.py:148
  26.3 1.9 %collective-permute-start.5 = (bf16[224,4096]{1,0:T(8,128)(2,1)}, bf16[224,4096]{1,0:T(8,128)(2,1)}, u32[]{:S(2)}, u32[]{:S(2)}) collective-permute-start(bf16[224,4096]{1,0:T(8,128)(2,1)} %refs_4_), channel_id=1, source_target_pairs={{0,1},{1,0},{2,3},{3,2},{4,5},{5,4},{6,7},{7,6},{8,9},{9,8},{10,11... | collective-permute-start | bytes 5505032 | tf_op jit(solution)/shard_map/ppermute | solution.py:148
  28.3 3.3 %collective-permute-start.1 = (bf16[256,384]{1,0:T(8,128)(2,1)}, bf16[256,384]{1,0:T(8,128)(2,1)S(1)}, u32[]{:S(2)}, u32[]{:S(2)}) collective-permute-start(bf16[256,384]{1,0:T(8,128)(2,1)} %get-tuple-element.15), channel_id=1, source_target_pairs={{0,384},{192,576},{384,0},{576,192},{1,385},{193,577},{385,1},{577... | collective-permute-start | bytes 589832 | tf_op jit(solution)/shard_map/ppermute | solution.py:148
  31.6 3.0 %collective-permute-start.2 = (bf16[256,384]{1,0:T(8,128)(2,1)}, bf16[256,384]{1,0:T(8,128)(2,1)S(1)}, u32[]{:S(2)}, u32[]{:S(2)}) collective-permute-start(bf16[256,384]{1,0:T(8,128)(2,1)} %get-tuple-element.16), channel_id=1, source_target_pairs={{0,576},{192,0},{384,192},{576,384},{1,577},{193,1},{385,193},{577... | collective-permute-start | bytes 589832 | tf_op jit(solution)/shard_map/ppermute | solution.py:148
  34.6 4.9 %collective-permute-done.1.refs_2_ = bf16[256,384]{1,0:T(8,128)(2,1)S(1)} collective-permute-done((bf16[256,384]{1,0:T(8,128)(2,1)}, bf16[256,384]{1,0:T(8,128)(2,1)S(1)}, u32[]{:S(2)}, u32[]{:S(2)}) %collective-permute-start.1) | collective-permute-done | bytes 196640 | tf_op jit(solution)/shard_map/ppermute | solution.py:148
  39.6 3.8 %collective-permute-done.2.refs_3_ = bf16[256,384]{1,0:T(8,128)(2,1)S(1)} collective-permute-done((bf16[256,384]{1,0:T(8,128)(2,1)}, bf16[256,384]{1,0:T(8,128)(2,1)S(1)}, u32[]{:S(2)}, u32[]{:S(2)}) %collective-permute-start.2) | collective-permute-done | bytes 196640 | tf_op jit(solution)/shard_map/ppermute | solution.py:148
  43.4 0.0 copy-start.1
  43.4 0.9 copy-done.1
  44.3 0.8 shard_map.88
  45.1 0.0 all-to-all-done.x_ref
  45.1 11.2 %all-to-all-start.1 = ((bf16[3,256,128]{2,1,0:T(8,128)(2,1)}), bf16[3,256,128]{2,1,0:T(8,128)(2,1)S(1)}, u32[]{:S(2)}, u32[]{:S(2)}) async-start(bf16[3,256,128]{2,1,0:T(8,128)(2,1)} %shard_map.88), calls=%async_computation.1 | async-start | bytes 393216 | tf_op jit(solution)/shard_map/all_to_all | solution.py:190
  56.3 0.0 collective-permute-done.3.refs_1_
  56.3 0.0 collective-permute-done.4.refs_3_
  56.3 0.0 collective-permute-done.5.refs_5_
  56.3 7.0 %shard_map.89 = bf16[32,8,2048]{2,1,0:T(8,128)(2,1)} custom-call(bf16[32,8,2048]{2,1,0:T(8,128)(2,1)S(1)} %all-to-all-done.x_ref, bf16[224,4096]{1,0:T(8,128)(2,1)S(1)} %bitcast.5, bf16[224,4096]{1,0:T(8,128)(2,1)} %collective-permute-done.3.refs_1_, bf16[224,4096]{1,0:T(8,128)(2,1)} %bitcast.7, bf16[224,4096]{1,0:T(8,128)(2,1)} %collective-permute-done.4.refs_3_, ...), custom_call_target="tpu_custom_call" | custom-call | flops 1409286144 | bytes 12845056 | tf_op jit(solution)/shard_map/pallas_call | solution.py:24
  63.3 0.0 copy-start.2
  63.3 0.0 copy-start.3
  63.4 2.5 %all-to-all-done.1.in_ref = bf16[3,256,128]{2,1,0:T(8,128)(2,1)S(1)} async-done(((bf16[3,256,128]{2,1,0:T(8,128)(2,1)}), bf16[3,256,128]{2,1,0:T(8,128)(2,1)S(1)}, u32[]{:S(2)}, u32[]{:S(2)}) %all-to-all-start.1) | async-done | bytes 196640 | tf_op jit(solution)/shard_map/all_to_all | solution.py:190
  65.9 12.3 %all-to-all-start.2 = ((bf16[32,8,2048]{2,1,0:T(8,128)(2,1)}), bf16[32,8,2048]{2,1,0:T(8,128)(2,1)S(1)}, u32[]{:S(2)}, u32[]{:S(2)}) async-start(bf16[32,8,2048]{2,1,0:T(8,128)(2,1)} %shard_map.89), calls=%async_computation.2 | async-start | bytes 2097152 | tf_op jit(solution)/shard_map/all_to_all | solution.py:198
  78.2 0.7 shard_map.91
  78.9 26.8 %all-to-all-done.2.in_ref = bf16[32,8,2048]{2,1,0:T(8,128)(2,1)S(1)} async-done(((bf16[32,8,2048]{2,1,0:T(8,128)(2,1)}), bf16[32,8,2048]{2,1,0:T(8,128)(2,1)S(1)}, u32[]{:S(2)}, u32[]{:S(2)}) %all-to-all-start.2) | async-done | bytes 1048608 | tf_op jit(solution)/shard_map/all_to_all | solution.py:198
  105.7 0.0 copy-done.2
  105.7 0.0 copy-done.3
  105.7 0.8 shard_map.90
Async XLA Ops:
  0.6 19.7 %copy-start = (bf16[4096,224]{0,1:T(8,128)(2,1)S(1)}, bf16[4096,224]{0,1:T(8,128)(2,1)}, u32[]{:S(2)}) copy-start(bf16[4096,224]{0,1:T(8,128)(2,1)} %param.9) | copy-start | bytes 5505028
  2.7 42.4 %all-to-all-start = ((bf16[32,8,2048]{2,1,0:T(8,128)(2,1)}), bf16[32,8,2048]{2,1,0:T(8,128)(2,1)S(1)}, u32[]{:S(2)}, u32[]{:S(2)}) async-start(bf16[32,8,2048]{2,1,0:T(8,128)(2,1)} %shard_map.86), calls=%async_computation | async-start | bytes 2097152 | tf_op jit(solution)/shard_map/all_to_all | solution.py:182
  17.9 8.5 %collective-permute-start = (bf16[256,384]{1,0:T(8,128)(2,1)}, bf16[256,384]{1,0:T(8,128)(2,1)S(1)}, u32[]{:S(2)}, u32[]{:S(2)}) collective-permute-start(bf16[256,384]{1,0:T(8,128)(2,1)} %get-tuple-element.13), channel_id=1, source_target_pairs={{0,192},{192,384},{384,576},{576,0},{1,193},{193,385},{385,577},{5... | collective-permute-start | bytes 589832 | tf_op jit(solution)/shard_map/ppermute | solution.py:148
  20.3 36.0 %collective-permute-start.3 = (bf16[224,4096]{1,0:T(8,128)(2,1)S(1)}, bf16[224,4096]{1,0:T(8,128)(2,1)}, u32[]{:S(2)}, u32[]{:S(2)}) collective-permute-start(bf16[224,4096]{1,0:T(8,128)(2,1)S(1)} %bitcast.4), channel_id=1, source_target_pairs={{0,1},{1,0},{2,3},{3,2},{4,5},{5,4},{6,7},{7,6},{8,9},{9,8},{10,11... | collective-permute-start | bytes 5505032 | tf_op jit(solution)/shard_map/ppermute | solution.py:148
  22.2 34.1 %collective-permute-start.4 = (bf16[224,4096]{1,0:T(8,128)(2,1)}, bf16[224,4096]{1,0:T(8,128)(2,1)}, u32[]{:S(2)}, u32[]{:S(2)}) collective-permute-start(bf16[224,4096]{1,0:T(8,128)(2,1)} %bitcast.6), channel_id=1, source_target_pairs={{0,1},{1,0},{2,3},{3,2},{4,5},{5,4},{6,7},{7,6},{8,9},{9,8},{10,11... | collective-permute-start | bytes 5505032 | tf_op jit(solution)/shard_map/ppermute | solution.py:148
  26.3 30.0 %collective-permute-start.5 = (bf16[224,4096]{1,0:T(8,128)(2,1)}, bf16[224,4096]{1,0:T(8,128)(2,1)}, u32[]{:S(2)}, u32[]{:S(2)}) collective-permute-start(bf16[224,4096]{1,0:T(8,128)(2,1)} %refs_4_), channel_id=1, source_target_pairs={{0,1},{1,0},{2,3},{3,2},{4,5},{5,4},{6,7},{7,6},{8,9},{9,8},{10,11... | collective-permute-start | bytes 5505032 | tf_op jit(solution)/shard_map/ppermute | solution.py:148
  28.3 11.3 %collective-permute-start.1 = (bf16[256,384]{1,0:T(8,128)(2,1)}, bf16[256,384]{1,0:T(8,128)(2,1)S(1)}, u32[]{:S(2)}, u32[]{:S(2)}) collective-permute-start(bf16[256,384]{1,0:T(8,128)(2,1)} %get-tuple-element.15), channel_id=1, source_target_pairs={{0,384},{192,576},{384,0},{576,192},{1,385},{193,577},{385,1},{577... | collective-permute-start | bytes 589832 | tf_op jit(solution)/shard_map/ppermute | solution.py:148
  31.6 11.8 %collective-permute-start.2 = (bf16[256,384]{1,0:T(8,128)(2,1)}, bf16[256,384]{1,0:T(8,128)(2,1)S(1)}, u32[]{:S(2)}, u32[]{:S(2)}) collective-permute-start(bf16[256,384]{1,0:T(8,128)(2,1)} %get-tuple-element.16), channel_id=1, source_target_pairs={{0,576},{192,0},{384,192},{576,384},{1,577},{193,1},{385,193},{577... | collective-permute-start | bytes 589832 | tf_op jit(solution)/shard_map/ppermute | solution.py:148
  43.4 0.9 copy-start.1
  45.1 20.8 %all-to-all-start.1 = ((bf16[3,256,128]{2,1,0:T(8,128)(2,1)}), bf16[3,256,128]{2,1,0:T(8,128)(2,1)S(1)}, u32[]{:S(2)}, u32[]{:S(2)}) async-start(bf16[3,256,128]{2,1,0:T(8,128)(2,1)} %shard_map.88), calls=%async_computation.1 | async-start | bytes 393216 | tf_op jit(solution)/shard_map/all_to_all | solution.py:190
  63.3 42.4 %copy-start.2 = (bf16[4,4096]{1,0:T(4,128)(2,1)S(1)}, bf16[4,4096]{1,0:T(4,128)(2,1)}, u32[]{:S(2)}) copy-start(bf16[4,4096]{1,0:T(4,128)(2,1)} %tok_ref.1) | copy-start | bytes 98308
  63.3 42.4 %copy-start.3 = (s32[4,4096]{1,0:T(4,128)S(1)}, s32[4,4096]{1,0:T(4,128)}, u32[]{:S(2)}) copy-start(s32[4,4096]{1,0:T(4,128)} %mask_ref.1) | copy-start | bytes 196612
  65.9 39.8 %all-to-all-start.2 = ((bf16[32,8,2048]{2,1,0:T(8,128)(2,1)}), bf16[32,8,2048]{2,1,0:T(8,128)(2,1)S(1)}, u32[]{:S(2)}, u32[]{:S(2)}) async-start(bf16[32,8,2048]{2,1,0:T(8,128)(2,1)} %shard_map.89), calls=%async_computation.2 | async-start | bytes 2097152 | tf_op jit(solution)/shard_map/all_to_all | solution.py:198

commit v4 on v2

--- a/solution.py
+++ b/solution.py
@@ -9,8 +9,8 @@
 from jax.sharding import PartitionSpec as P
 
 DP = ("x", "zh")
-CHIPS = ("y", "zl")
-TENSOR = CHIPS + ("c",)
+CHIPS = ("y", "zb", "za")
+TENSOR = ("y", "za", "zb", "c")
 BF16, F32 = jnp.bfloat16, jnp.float32
 EPS = 1e-05
 KEEP = 0.9
@@ -94,12 +94,10 @@
         out_ref[:, :, k * step : (k + 1) * step] = both.reshape(blocks, eight, step).astype(BF16)
 
 
-def final_body(in_ref, tok_ref, mask_ref, out_ref):
+def final_body(kept_ref, come_ref, tok_ref, mask_ref, out_ref):
     few, wide = tok_ref.shape
     half = wide // 2
-    total = in_ref[0].astype(F32)
-    for i in range(1, in_ref.shape[0]):
-        total = total + in_ref[i].astype(F32)
+    total = kept_ref[...] + come_ref[...].astype(F32)
     for q in range(2):
         cols = slice(q * half, (q + 1) * half)
         branch = total[q * few : (q + 1) * few]
@@ -130,13 +128,14 @@
         out[...] = held[:, pl.ds(pl.multiple_of(at, width), width)].astype(out.dtype)
 
 
-def sum_first_body(in_ref, out_ref):
-    rows = 16
-    for r in range(0, out_ref.shape[0], rows):
-        total = in_ref[0, r : r + rows].astype(F32)
-        for i in range(1, in_ref.shape[0]):
-            total = total + in_ref[i, r : r + rows].astype(F32)
-        out_ref[r : r + rows] = total.astype(BF16)
+def sum_first_body(place_ref, in_ref, kept_ref, sent_ref):
+    total = in_ref[0].astype(F32)
+    for i in range(1, in_ref.shape[0]):
+        total = total + in_ref[i].astype(F32)
+    rows = kept_ref.shape[0]
+    first = place_ref[0] == 0
+    kept_ref[...] = jnp.where(first, total[:rows], total[rows:])
+    sent_ref[...] = jnp.where(first, total[rows:], total[:rows]).astype(BF16)
 
 
 def sum_body(*refs):
@@ -210,19 +209,24 @@
         vmem=48, flops=12 * chips * few * wide * units, moved=14 * wide * units,
     )
     bucket = [cut[0]] + [passed_on(cut[k], "zh", k) for k in range(1, len(cut))]
-    ny, nz = (lax.axis_size(axis) for axis in CHIPS)
-    terms = terms.reshape(ny, nz * 2 * few, wide // 2)
-    terms = lax.all_to_all(terms, "y", 0, 0, tiled=True)
-    terms = call(sum_first_body, shape(nz * 2 * few, wide // 2), terms)
-    terms, bucket = lax.optimization_barrier((terms.reshape(nz, 2 * few, wide // 2), bucket))
-    terms = lax.all_to_all(terms, "zl", 0, 0, tiled=True)
+    pairs = lax.axis_size(("y", "zb"))
+    terms = terms.reshape(pairs, 4 * few, wide // 2)
+    terms = lax.all_to_all(terms, ("y", "zb"), 0, 0, tiled=True)
+    kept, sent = call(
+        sum_first_body,
+        (shape(2 * few, wide // 2, dtype=F32), shape(2 * few, wide // 2)),
+        place("za"), terms,
+        smem=1,
+    )
+    sent, bucket = lax.optimization_barrier((sent, bucket))
+    come = passed_on(sent, "za", 1)
     reduced = call(sum_body, shape(*cut[0].shape, dtype=F32), *bucket)
-    mixed = call(final_body, shape(few, wide), terms, tokens, drop_mask)
+    mixed = call(final_body, shape(few, wide), kept, come, tokens, drop_mask)
     return (mixed, reduced)
 
 
 def solution(mesh):
-    finer = Mesh(mesh.devices.reshape(4, 3, 8, 4, 2), DP + TENSOR)
+    finer = Mesh(mesh.devices.reshape(4, 3, 8, 2, 2, 2), DP + TENSOR)
     return jax.shard_map(
         per_device,
         mesh=finer,

time: 101 us -> 101 us (level)
    ppermute x8 -> x9, waiting for transfers between devices: 10.4 us -> 17.4 us  [passed_on(): return lax.ppermute(x, axis, [(i, (i + by) % size) for i in range(size)])]
    all_to_all x2 -> x1, waiting for transfers between devices: 20.6 us -> 13.9 us  [per_device(): terms = lax.all_to_all(terms, ('y', 'zb'), 0, 0, tiled=True)]
    all_to_all x2 -> x1, starting transfers between devices: 11.4 us -> 7.85 us  [per_device(): terms = lax.all_to_all(terms, ('y', 'zb'), 0, 0, tiled=True)]
    ppermute x8 -> x9, starting transfers between devices: 28.8 us -> 31.8 us  [passed_on(): return lax.ppermute(x, axis, [(i, (i + by) % size) for i in range(size)])]
  transfers between devices with their start and end apart: 11 -> 11, of which waited for: 5 -> 6; matrix products, arithmetic and copies ran while one was open for 0% -> 0% of each run, Pallas kernels for 4% -> 3%
where the time goes in v4:
time: 101 us; the launch traced here: 99.9 us
  starting transfers between devices  52.6 us (52%)
  waiting for transfers between devices  31.4 us (31%)
  Pallas kernels  12.9 us (13%)
  local copies, waits for them, and re-layouts  2.19 us (2%)
    ppermute x9, starting transfers between devices, passed_on(): return lax.ppermute(x, axis, [(i, (i + by) % size) for i in range(size)])  31.8 us
    ppermute x9, waiting for transfers between devices, passed_on(): return lax.ppermute(x, axis, [(i, (i + by) % size) for i in range(size)])  17.4 us
    all_to_all x1, waiting for transfers between devices, per_device(): terms = lax.all_to_all(terms, ('y', 'zb'), 0, 0, tiled=True)  13.9 us
    all_to_all x1, starting transfers between devices, per_device(): gathered = lax.all_to_all(gathered, CHIPS, 0, 0, tiled=True)  12.9 us
    pallas_call x7, Pallas kernels, call(): pl.pallas_call(body, out_shape=outs, in_specs=specs, out_specs=jax.tree.m...  12.9 us
    all_to_all x1, starting transfers between devices, per_device(): terms = lax.all_to_all(terms, ('y', 'zb'), 0, 0, tiled=True)  7.85 us
    unnamed x16, local copies, waits for them, and re-layouts  2.19 us
  transfers between devices with their start and end apart: 11, of which 6 were waited for; matrix products, arithmetic and copies ran while one was open for 0% of the time, Pallas kernels for 3%

profile of v4, /device:TPU:6, one launch (start us, length us, event | category | flops | bytes accessed | tf_op | source)
XLA Modules:
  0.0 99.9 jit_solution(13620028482309642825)
XLA Ops:
  0.6 0.0 copy-start
  0.6 2.1 %shard_map.86 = bf16[32,8,2048]{2,1,0:T(8,128)(2,1)} custom-call(bf16[4,4096]{1,0:T(4,128)(2,1)} %tok_ref.1, bf16[4096]{0:T(1024)(128)(2,1)} %gain_hbm.1), custom_call_target="tpu_custom_call" | custom-call | bytes 1048576 | tf_op jit(solution)/shard_map/pallas_call | solution.py:24
  2.8 12.9 %all-to-all-start = ((bf16[32,8,2048]{2,1,0:T(8,128)(2,1)}), bf16[32,8,2048]{2,1,0:T(8,128)(2,1)S(1)}, u32[]{:S(2)}, u32[]{:S(2)}) async-start(bf16[32,8,2048]{2,1,0:T(8,128)(2,1)} %shard_map.86), calls=%async_computation | async-start | bytes 2097152 | tf_op jit(solution)/shard_map/all_to_all | solution.py:197
  15.7 2.2 %shard_map.87 = (bf16[256,384]{1,0:T(8,128)(2,1)}, bf16[256,384]{1,0:T(8,128)(2,1)}, bf16[256,384]{1,0:T(8,128)(2,1)}, bf16[256,384]{1,0:T(8,128)(2,1)}) custom-call(s32[1]{0:T(128)} %bitcast.2.place_ref, bf16[256,1536]{1,0:T(8,128)(2,1)} %bitcast.11), custom_call_target="tpu_custom_call" | custom-call | bytes 1048576 | tf_op jit(solution)/shard_map/pallas_call | solution.py:24
  17.9 2.4 %collective-permute-start = (bf16[256,384]{1,0:T(8,128)(2,1)}, bf16[256,384]{1,0:T(8,128)(2,1)S(1)}, u32[]{:S(2)}, u32[]{:S(2)}) collective-permute-start(bf16[256,384]{1,0:T(8,128)(2,1)} %get-tuple-element.22), channel_id=1, source_target_pairs={{0,192},{192,384},{384,576},{576,0},{1,193},{193,385},{385,577},{5... | collective-permute-start | bytes 589832 | tf_op jit(solution)/shard_map/ppermute | solution.py:158
  20.3 0.0 copy-done
  20.3 1.9 %collective-permute-start.3 = (bf16[224,4096]{1,0:T(8,128)(2,1)S(1)}, bf16[224,4096]{1,0:T(8,128)(2,1)}, u32[]{:S(2)}, u32[]{:S(2)}) collective-permute-start(bf16[224,4096]{1,0:T(8,128)(2,1)S(1)} %bitcast.7), channel_id=1, source_target_pairs={{0,1},{1,0},{2,3},{3,2},{4,5},{5,4},{6,7},{7,6},{8,9},{9,8},{10,11... | collective-permute-start | bytes 5505032 | tf_op jit(solution)/shard_map/ppermute | solution.py:158
  22.2 2.4 %collective-permute-start.4 = (bf16[224,4096]{1,0:T(8,128)(2,1)}, bf16[224,4096]{1,0:T(8,128)(2,1)}, u32[]{:S(2)}, u32[]{:S(2)}) collective-permute-start(bf16[224,4096]{1,0:T(8,128)(2,1)} %bitcast.9), channel_id=1, source_target_pairs={{0,1},{1,0},{2,3},{3,2},{4,5},{5,4},{6,7},{7,6},{8,9},{9,8},{10,11... | collective-permute-start | bytes 5505032 | tf_op jit(solution)/shard_map/ppermute | solution.py:158
  24.6 1.7 %collective-permute-done.refs_1_ = bf16[256,384]{1,0:T(8,128)(2,1)S(1)} collective-permute-done((bf16[256,384]{1,0:T(8,128)(2,1)}, bf16[256,384]{1,0:T(8,128)(2,1)S(1)}, u32[]{:S(2)}, u32[]{:S(2)}) %collective-permute-start) | collective-permute-done | bytes 196640 | tf_op jit(solution)/shard_map/ppermute | solution.py:158
  26.3 1.9 %collective-permute-start.5 = (bf16[224,4096]{1,0:T(8,128)(2,1)}, bf16[224,4096]{1,0:T(8,128)(2,1)}, u32[]{:S(2)}, u32[]{:S(2)}) collective-permute-start(bf16[224,4096]{1,0:T(8,128)(2,1)} %refs_4_), channel_id=1, source_target_pairs={{0,1},{1,0},{2,3},{3,2},{4,5},{5,4},{6,7},{7,6},{8,9},{9,8},{10,11... | collective-permute-start | bytes 5505032 | tf_op jit(solution)/shard_map/ppermute | solution.py:158
  28.3 3.3 %collective-permute-start.1 = (bf16[256,384]{1,0:T(8,128)(2,1)}, bf16[256,384]{1,0:T(8,128)(2,1)S(1)}, u32[]{:S(2)}, u32[]{:S(2)}) collective-permute-start(bf16[256,384]{1,0:T(8,128)(2,1)} %get-tuple-element.24), channel_id=1, source_target_pairs={{0,384},{192,576},{384,0},{576,192},{1,385},{193,577},{385,1},{577... | collective-permute-start | bytes 589832 | tf_op jit(solution)/shard_map/ppermute | solution.py:158
  31.6 3.0 %collective-permute-start.2 = (bf16[256,384]{1,0:T(8,128)(2,1)}, bf16[256,384]{1,0:T(8,128)(2,1)S(1)}, u32[]{:S(2)}, u32[]{:S(2)}) collective-permute-start(bf16[256,384]{1,0:T(8,128)(2,1)} %get-tuple-element.25), channel_id=1, source_target_pairs={{0,576},{192,0},{384,192},{576,384},{1,577},{193,1},{385,193},{577... | collective-permute-start | bytes 589832 | tf_op jit(solution)/shard_map/ppermute | solution.py:158
  34.6 4.9 %collective-permute-done.1.refs_2_ = bf16[256,384]{1,0:T(8,128)(2,1)S(1)} collective-permute-done((bf16[256,384]{1,0:T(8,128)(2,1)}, bf16[256,384]{1,0:T(8,128)(2,1)S(1)}, u32[]{:S(2)}, u32[]{:S(2)}) %collective-permute-start.1) | collective-permute-done | bytes 196640 | tf_op jit(solution)/shard_map/ppermute | solution.py:158
  39.6 3.8 %collective-permute-done.2.refs_3_ = bf16[256,384]{1,0:T(8,128)(2,1)S(1)} collective-permute-done((bf16[256,384]{1,0:T(8,128)(2,1)}, bf16[256,384]{1,0:T(8,128)(2,1)S(1)}, u32[]{:S(2)}, u32[]{:S(2)}) %collective-permute-start.2) | collective-permute-done | bytes 196640 | tf_op jit(solution)/shard_map/ppermute | solution.py:158
  43.4 0.0 copy-start.1
  43.4 0.9 copy-done.1
  44.3 0.2 shard_map.88
  44.5 0.0 copy-start.4
  44.5 0.6 copy-done.4
  45.1 0.0 copy-start.6
  45.1 0.6 copy-done.6
  45.7 0.0 all-to-all-done.x_ref
  45.7 0.0 collective-permute-done.3.refs_1_
  45.7 0.0 collective-permute-done.4.refs_3_
  45.7 0.0 collective-permute-done.5.refs_5_
  45.7 7.0 %shard_map.89 = bf16[32,8,2048]{2,1,0:T(8,128)(2,1)} custom-call(bf16[32,8,2048]{2,1,0:T(8,128)(2,1)S(1)} %all-to-all-done.x_ref, bf16[224,4096]{1,0:T(8,128)(2,1)S(1)} %bitcast.8, bf16[224,4096]{1,0:T(8,128)(2,1)} %collective-permute-done.3.refs_1_, bf16[224,4096]{1,0:T(8,128)(2,1)} %bitcast.10, bf16[224,4096]{1,0:T(8,128)(2,1)} %collective-permute-done.4.refs_3_, ...), custom_call_target="tpu_custom_call" | custom-call | flops 1409286144 | bytes 12845056 | tf_op jit(solution)/shard_map/pallas_call | solution.py:24
  52.8 0.0 copy-start.7
  52.8 0.0 copy-start.5
  52.8 0.0 copy-start.2
  52.8 0.0 copy-start.3
  52.8 7.8 %all-to-all-start.1 = ((bf16[16,16,2048]{2,1,0:T(8,128)(2,1)}), bf16[16,16,2048]{2,1,0:T(8,128)(2,1)S(1)}, u32[]{:S(2)}, u32[]{:S(2)}) async-start(bf16[16,16,2048]{2,1,0:T(8,128)(2,1)} %bitcast.6), calls=%async_computation.1 | async-start | bytes 2097152 | tf_op jit(solution)/shard_map/all_to_all | solution.py:214
  60.7 0.0 copy-done.7
  60.7 10.6 %collective-permute-start.6 = (bf16[256,128]{1,0:T(8,128)(2,1)S(1)}, bf16[256,128]{1,0:T(8,128)(2,1)S(1)}, u32[]{:S(2)}, u32[]{:S(2)}) collective-permute-start(bf16[256,128]{1,0:T(8,128)(2,1)S(1)} %copy-done.7), channel_id=1, source_target_pairs={{0,64},{64,128},{128,0},{1,65},{65,129},{129,1},{2,66},{66,130},{1... | collective-permute-start | bytes 196616 | tf_op jit(solution)/shard_map/ppermute | solution.py:158
  71.3 0.0 copy-done.5
  71.3 3.1 %collective-permute-start.7 = (bf16[256,128]{1,0:T(8,128)(2,1)S(1)}, bf16[256,128]{1,0:T(8,128)(2,1)S(1)}, u32[]{:S(2)}, u32[]{:S(2)}) collective-permute-start(bf16[256,128]{1,0:T(8,128)(2,1)S(1)} %copy-done.5), channel_id=1, source_target_pairs={{0,128},{64,0},{128,64},{1,129},{65,1},{129,65},{2,130},{66,2},{13... | collective-permute-start | bytes 196616 | tf_op jit(solution)/shard_map/ppermute | solution.py:158
  74.5 13.9 %all-to-all-done.1.in_ref = bf16[16,16,2048]{2,1,0:T(8,128)(2,1)S(1)} async-done(((bf16[16,16,2048]{2,1,0:T(8,128)(2,1)}), bf16[16,16,2048]{2,1,0:T(8,128)(2,1)S(1)}, u32[]{:S(2)}, u32[]{:S(2)}) %all-to-all-start.1) | async-done | bytes 1048608 | tf_op jit(solution)/shard_map/all_to_all | solution.py:214
  88.4 0.1 shard_map.90
  88.6 4.0 %collective-permute-done.6.refs_1_ = bf16[256,128]{1,0:T(8,128)(2,1)S(1)} collective-permute-done((bf16[256,128]{1,0:T(8,128)(2,1)S(1)}, bf16[256,128]{1,0:T(8,128)(2,1)S(1)}, u32[]{:S(2)}, u32[]{:S(2)}) %collective-permute-start.6) | collective-permute-done | bytes 65568 | tf_op jit(solution)/shard_map/ppermute | solution.py:158
  92.5 0.0 collective-permute-done.7.refs_2_
  92.5 3.0 %collective-permute-start.8 = (bf16[8,2048]{1,0:T(8,128)(2,1)S(1)}, bf16[8,2048]{1,0:T(8,128)(2,1)S(1)}, u32[]{:S(2)}, u32[]{:S(2)}) collective-permute-start(bf16[8,2048]{1,0:T(8,128)(2,1)S(1)} %get-tuple-element.36), channel_id=1, source_target_pairs={{0,4},{4,0},{1,5},{5,1},{2,6},{6,2},{3,7},{7,3},{8,12},{12,8},{9,1... | collective-permute-start | bytes 98312 | tf_op jit(solution)/shard_map/ppermute | solution.py:158
  95.5 0.7 shard_map.92
  96.2 3.0 %collective-permute-done.8.come_ref = bf16[8,2048]{1,0:T(8,128)(2,1)S(1)} collective-permute-done((bf16[8,2048]{1,0:T(8,128)(2,1)S(1)}, bf16[8,2048]{1,0:T(8,128)(2,1)S(1)}, u32[]{:S(2)}, u32[]{:S(2)}) %collective-permute-start.8) | collective-permute-done | bytes 32800 | tf_op jit(solution)/shard_map/ppermute | solution.py:158
  99.2 0.0 copy-done.2
  99.2 0.0 copy-done.3
  99.2 0.6 shard_map.91
Async XLA Ops:
  0.6 19.7 %copy-start = (bf16[4096,224]{0,1:T(8,128)(2,1)S(1)}, bf16[4096,224]{0,1:T(8,128)(2,1)}, u32[]{:S(2)}) copy-start(bf16[4096,224]{0,1:T(8,128)(2,1)} %param.9) | copy-start | bytes 5505028
  2.8 43.0 %all-to-all-start = ((bf16[32,8,2048]{2,1,0:T(8,128)(2,1)}), bf16[32,8,2048]{2,1,0:T(8,128)(2,1)S(1)}, u32[]{:S(2)}, u32[]{:S(2)}) async-start(bf16[32,8,2048]{2,1,0:T(8,128)(2,1)} %shard_map.86), calls=%async_computation | async-start | bytes 2097152 | tf_op jit(solution)/shard_map/all_to_all | solution.py:197
  17.9 8.5 %collective-permute-start = (bf16[256,384]{1,0:T(8,128)(2,1)}, bf16[256,384]{1,0:T(8,128)(2,1)S(1)}, u32[]{:S(2)}, u32[]{:S(2)}) collective-permute-start(bf16[256,384]{1,0:T(8,128)(2,1)} %get-tuple-element.22), channel_id=1, source_target_pairs={{0,192},{192,384},{384,576},{576,0},{1,193},{193,385},{385,577},{5... | collective-permute-start | bytes 589832 | tf_op jit(solution)/shard_map/ppermute | solution.py:158
  20.3 25.4 %collective-permute-start.3 = (bf16[224,4096]{1,0:T(8,128)(2,1)S(1)}, bf16[224,4096]{1,0:T(8,128)(2,1)}, u32[]{:S(2)}, u32[]{:S(2)}) collective-permute-start(bf16[224,4096]{1,0:T(8,128)(2,1)S(1)} %bitcast.7), channel_id=1, source_target_pairs={{0,1},{1,0},{2,3},{3,2},{4,5},{5,4},{6,7},{7,6},{8,9},{9,8},{10,11... | collective-permute-start | bytes 5505032 | tf_op jit(solution)/shard_map/ppermute | solution.py:158
  22.2 23.5 %collective-permute-start.4 = (bf16[224,4096]{1,0:T(8,128)(2,1)}, bf16[224,4096]{1,0:T(8,128)(2,1)}, u32[]{:S(2)}, u32[]{:S(2)}) collective-permute-start(bf16[224,4096]{1,0:T(8,128)(2,1)} %bitcast.9), channel_id=1, source_target_pairs={{0,1},{1,0},{2,3},{3,2},{4,5},{5,4},{6,7},{7,6},{8,9},{9,8},{10,11... | collective-permute-start | bytes 5505032 | tf_op jit(solution)/shard_map/ppermute | solution.py:158
  26.3 19.4 %collective-permute-start.5 = (bf16[224,4096]{1,0:T(8,128)(2,1)}, bf16[224,4096]{1,0:T(8,128)(2,1)}, u32[]{:S(2)}, u32[]{:S(2)}) collective-permute-start(bf16[224,4096]{1,0:T(8,128)(2,1)} %refs_4_), channel_id=1, source_target_pairs={{0,1},{1,0},{2,3},{3,2},{4,5},{5,4},{6,7},{7,6},{8,9},{9,8},{10,11... | collective-permute-start | bytes 5505032 | tf_op jit(solution)/shard_map/ppermute | solution.py:158
  28.3 11.3 %collective-permute-start.1 = (bf16[256,384]{1,0:T(8,128)(2,1)}, bf16[256,384]{1,0:T(8,128)(2,1)S(1)}, u32[]{:S(2)}, u32[]{:S(2)}) collective-permute-start(bf16[256,384]{1,0:T(8,128)(2,1)} %get-tuple-element.24), channel_id=1, source_target_pairs={{0,384},{192,576},{384,0},{576,192},{1,385},{193,577},{385,1},{577... | collective-permute-start | bytes 589832 | tf_op jit(solution)/shard_map/ppermute | solution.py:158
  31.6 11.8 %collective-permute-start.2 = (bf16[256,384]{1,0:T(8,128)(2,1)}, bf16[256,384]{1,0:T(8,128)(2,1)S(1)}, u32[]{:S(2)}, u32[]{:S(2)}) collective-permute-start(bf16[256,384]{1,0:T(8,128)(2,1)} %get-tuple-element.25), channel_id=1, source_target_pairs={{0,576},{192,0},{384,192},{576,384},{1,577},{193,1},{385,193},{577... | collective-permute-start | bytes 589832 | tf_op jit(solution)/shard_map/ppermute | solution.py:158
  43.4 0.9 copy-start.1
  44.5 0.6 copy-start.4
  45.1 0.6 copy-start.6
  52.8 7.9 %copy-start.7 = (bf16[256,128]{1,0:T(8,128)(2,1)S(1)}, bf16[256,128]{1,0:T(8,128)(2,1)}, u32[]{:S(2)}) copy-start(bf16[256,128]{1,0:T(8,128)(2,1)} %copy-done.6) | copy-start | bytes 196612
  52.8 18.5 %copy-start.5 = (bf16[256,128]{1,0:T(8,128)(2,1)S(1)}, bf16[256,128]{1,0:T(8,128)(2,1)}, u32[]{:S(2)}) copy-start(bf16[256,128]{1,0:T(8,128)(2,1)} %copy-done.4) | copy-start | bytes 196612
  52.8 46.4 %copy-start.2 = (bf16[4,4096]{1,0:T(4,128)(2,1)S(1)}, bf16[4,4096]{1,0:T(4,128)(2,1)}, u32[]{:S(2)}) copy-start(bf16[4,4096]{1,0:T(4,128)(2,1)} %tok_ref.1) | copy-start | bytes 98308
  52.8 46.4 %copy-start.3 = (s32[4,4096]{1,0:T(4,128)S(1)}, s32[4,4096]{1,0:T(4,128)}, u32[]{:S(2)}) copy-start(s32[4,4096]{1,0:T(4,128)} %mask_ref.1) | copy-start | bytes 196612
  52.8 35.6 %all-to-all-start.1 = ((bf16[16,16,2048]{2,1,0:T(8,128)(2,1)}), bf16[16,16,2048]{2,1,0:T(8,128)(2,1)S(1)}, u32[]{:S(2)}, u32[]{:S(2)}) async-start(bf16[16,16,2048]{2,1,0:T(8,128)(2,1)} %bitcast.6), calls=%async_computation.1 | async-start | bytes 2097152 | tf_op jit(solution)/shard_map/all_to_all | solution.py:214
  60.7 31.9 %collective-permute-start.6 = (bf16[256,128]{1,0:T(8,128)(2,1)S(1)}, bf16[256,128]{1,0:T(8,128)(2,1)S(1)}, u32[]{:S(2)}, u32[]{:S(2)}) collective-permute-start(bf16[256,128]{1,0:T(8,128)(2,1)S(1)} %copy-done.7), channel_id=1, source_target_pairs={{0,64},{64,128},{128,0},{1,65},{65,129},{129,1},{2,66},{66,130},{1... | collective-permute-start | bytes 196616 | tf_op jit(solution)/shard_map/ppermute | solution.py:158
  71.3 21.2 %collective-permute-start.7 = (bf16[256,128]{1,0:T(8,128)(2,1)S(1)}, bf16[256,128]{1,0:T(8,128)(2,1)S(1)}, u32[]{:S(2)}, u32[]{:S(2)}) collective-permute-start(bf16[256,128]{1,0:T(8,128)(2,1)S(1)} %copy-done.5), channel_id=1, source_target_pairs={{0,128},{64,0},{128,64},{1,129},{65,1},{129,65},{2,130},{66,2},{13... | collective-permute-start | bytes 196616 | tf_op jit(solution)/shard_map/ppermute | solution.py:158
  92.5 6.7 %collective-permute-start.8 = (bf16[8,2048]{1,0:T(8,128)(2,1)S(1)}, bf16[8,2048]{1,0:T(8,128)(2,1)S(1)}, u32[]{:S(2)}, u32[]{:S(2)}) collective-permute-start(bf16[8,2048]{1,0:T(8,128)(2,1)S(1)} %get-tuple-element.36), channel_id=1, source_target_pairs={{0,4},{4,0},{1,5},{5,1},{2,6},{6,2},{3,7},{7,3},{8,12},{12,8},{9,1... | collective-permute-start | bytes 98312 | tf_op jit(solution)/shard_map/ppermute | solution.py:158

commit v5 on v4

--- a/solution.py
+++ b/solution.py
@@ -218,7 +218,7 @@
         place("za"), terms,
         smem=1,
     )
-    sent, bucket = lax.optimization_barrier((sent, bucket))
+    sent, bucket[-1] = lax.optimization_barrier((sent, bucket[-1]))
     come = passed_on(sent, "za", 1)
     reduced = call(sum_body, shape(*cut[0].shape, dtype=F32), *bucket)
     mixed = call(final_body, shape(few, wide), kept, come, tokens, drop_mask)

time: 101 us -> 98.8 us (0.978)
  the two profiles are of different devices: /device:TPU:6 before, /device:TPU:122 now
where the time goes in v5:
time: 98.8 us; the launch traced here: 98.2 us
  starting transfers between devices  57 us (58%)
  waiting for transfers between devices  25.2 us (26%)
  Pallas kernels  12.9 us (13%)
  local copies, waits for them, and re-layouts  2.2 us (2%)
    ppermute x9, starting transfers between devices, passed_on(): return lax.ppermute(x, axis, [(i, (i + by) % size) for i in range(size)])  37.2 us
    ppermute x9, waiting for transfers between devices, passed_on(): return lax.ppermute(x, axis, [(i, (i + by) % size) for i in range(size)])  14.7 us
    pallas_call x7, Pallas kernels, call(): pl.pallas_call(body, out_shape=outs, in_specs=specs, out_specs=jax.tree.m...  12.9 us
    all_to_all x1, starting transfers between devices, per_device(): gathered = lax.all_to_all(gathered, CHIPS, 0, 0, tiled=True)  11.6 us
    all_to_all x1, waiting for transfers between devices, per_device(): terms = lax.all_to_all(terms, ('y', 'zb'), 0, 0, tiled=True)  10.6 us
    all_to_all x1, starting transfers between devices, per_device(): terms = lax.all_to_all(terms, ('y', 'zb'), 0, 0, tiled=True)  8.19 us
    unnamed x16, local copies, waits for them, and re-layouts  2.2 us
  transfers between devices with their start and end apart: 11, of which 6 were waited for; matrix products, arithmetic and copies ran while one was open for 0% of the time, Pallas kernels for 3%

profile of v5, /device:TPU:122, one launch (start us, length us, event | category | flops | bytes accessed | tf_op | source)
XLA Modules:
  0.0 98.2 jit_solution(16247348090013349080)
XLA Ops:
  0.6 0.0 copy-start
  0.6 2.1 %shard_map.86 = bf16[32,8,2048]{2,1,0:T(8,128)(2,1)} custom-call(bf16[4,4096]{1,0:T(4,128)(2,1)} %tok_ref.1, bf16[4096]{0:T(1024)(128)(2,1)} %gain_hbm.1), custom_call_target="tpu_custom_call" | custom-call | bytes 1048576 | tf_op jit(solution)/shard_map/pallas_call | solution.py:24
  2.8 11.6 %all-to-all-start = ((bf16[32,8,2048]{2,1,0:T(8,128)(2,1)}), bf16[32,8,2048]{2,1,0:T(8,128)(2,1)S(1)}, u32[]{:S(2)}, u32[]{:S(2)}) async-start(bf16[32,8,2048]{2,1,0:T(8,128)(2,1)} %shard_map.86), calls=%async_computation | async-start | bytes 2097152 | tf_op jit(solution)/shard_map/all_to_all | solution.py:197
  14.4 2.2 %shard_map.87 = (bf16[256,384]{1,0:T(8,128)(2,1)}, bf16[256,384]{1,0:T(8,128)(2,1)}, bf16[256,384]{1,0:T(8,128)(2,1)}, bf16[256,384]{1,0:T(8,128)(2,1)}) custom-call(s32[1]{0:T(128)} %bitcast.2.place_ref, bf16[256,1536]{1,0:T(8,128)(2,1)} %bitcast.11), custom_call_target="tpu_custom_call" | custom-call | bytes 1048576 | tf_op jit(solution)/shard_map/pallas_call | solution.py:24
  16.6 3.4 %collective-permute-start = (bf16[256,384]{1,0:T(8,128)(2,1)}, bf16[256,384]{1,0:T(8,128)(2,1)S(1)}, u32[]{:S(2)}, u32[]{:S(2)}) collective-permute-start(bf16[256,384]{1,0:T(8,128)(2,1)} %get-tuple-element.20), channel_id=1, source_target_pairs={{0,192},{192,384},{384,576},{576,0},{1,193},{193,385},{385,577},{5... | collective-permute-start | bytes 589832 | tf_op jit(solution)/shard_map/ppermute | solution.py:158
  20.0 0.0 copy-done
  20.0 1.9 %collective-permute-start.3 = (bf16[224,4096]{1,0:T(8,128)(2,1)S(1)}, bf16[224,4096]{1,0:T(8,128)(2,1)}, u32[]{:S(2)}, u32[]{:S(2)}) collective-permute-start(bf16[224,4096]{1,0:T(8,128)(2,1)S(1)} %bitcast.7), channel_id=1, source_target_pairs={{0,1},{1,0},{2,3},{3,2},{4,5},{5,4},{6,7},{7,6},{8,9},{9,8},{10,11... | collective-permute-start | bytes 5505032 | tf_op jit(solution)/shard_map/ppermute | solution.py:158
  21.9 2.4 %collective-permute-start.4 = (bf16[224,4096]{1,0:T(8,128)(2,1)}, bf16[224,4096]{1,0:T(8,128)(2,1)}, u32[]{:S(2)}, u32[]{:S(2)}) collective-permute-start(bf16[224,4096]{1,0:T(8,128)(2,1)} %bitcast.9), channel_id=1, source_target_pairs={{0,1},{1,0},{2,3},{3,2},{4,5},{5,4},{6,7},{7,6},{8,9},{9,8},{10,11... | collective-permute-start | bytes 5505032 | tf_op jit(solution)/shard_map/ppermute | solution.py:158
  24.3 0.4 collective-permute-done.refs_1_
  24.8 1.9 %collective-permute-start.5 = (bf16[224,4096]{1,0:T(8,128)(2,1)}, bf16[224,4096]{1,0:T(8,128)(2,1)}, u32[]{:S(2)}, u32[]{:S(2)}) collective-permute-start(bf16[224,4096]{1,0:T(8,128)(2,1)} %refs_4_), channel_id=1, source_target_pairs={{0,1},{1,0},{2,3},{3,2},{4,5},{5,4},{6,7},{7,6},{8,9},{9,8},{10,11... | collective-permute-start | bytes 5505032 | tf_op jit(solution)/shard_map/ppermute | solution.py:158
  26.7 4.0 %collective-permute-start.1 = (bf16[256,384]{1,0:T(8,128)(2,1)}, bf16[256,384]{1,0:T(8,128)(2,1)S(1)}, u32[]{:S(2)}, u32[]{:S(2)}) collective-permute-start(bf16[256,384]{1,0:T(8,128)(2,1)} %get-tuple-element.22), channel_id=1, source_target_pairs={{0,384},{192,576},{384,0},{576,192},{1,385},{193,577},{385,1},{577... | collective-permute-start | bytes 589832 | tf_op jit(solution)/shard_map/ppermute | solution.py:158
  30.7 3.3 %collective-permute-start.2 = (bf16[256,384]{1,0:T(8,128)(2,1)}, bf16[256,384]{1,0:T(8,128)(2,1)S(1)}, u32[]{:S(2)}, u32[]{:S(2)}) collective-permute-start(bf16[256,384]{1,0:T(8,128)(2,1)} %get-tuple-element.23), channel_id=1, source_target_pairs={{0,576},{192,0},{384,192},{576,384},{1,577},{193,1},{385,193},{577... | collective-permute-start | bytes 589832 | tf_op jit(solution)/shard_map/ppermute | solution.py:158
  34.1 3.9 %collective-permute-done.1.refs_2_ = bf16[256,384]{1,0:T(8,128)(2,1)S(1)} collective-permute-done((bf16[256,384]{1,0:T(8,128)(2,1)}, bf16[256,384]{1,0:T(8,128)(2,1)S(1)}, u32[]{:S(2)}, u32[]{:S(2)}) %collective-permute-start.1) | collective-permute-done | bytes 196640 | tf_op jit(solution)/shard_map/ppermute | solution.py:158
  38.0 3.8 %collective-permute-done.2.refs_3_ = bf16[256,384]{1,0:T(8,128)(2,1)S(1)} collective-permute-done((bf16[256,384]{1,0:T(8,128)(2,1)}, bf16[256,384]{1,0:T(8,128)(2,1)S(1)}, u32[]{:S(2)}, u32[]{:S(2)}) %collective-permute-start.2) | collective-permute-done | bytes 196640 | tf_op jit(solution)/shard_map/ppermute | solution.py:158
  41.8 0.0 copy-start.1
  41.8 0.9 copy-done.1
  42.7 0.2 shard_map.88
  42.9 0.0 copy-start.4
  42.9 0.6 copy-done.4
  43.5 0.0 copy-start.6
  43.5 0.6 copy-done.6
  44.1 0.0 all-to-all-done.x_ref
  44.1 0.0 collective-permute-done.3.refs_1_
  44.1 0.0 collective-permute-done.4.refs_3_
  44.2 0.0 collective-permute-done.5.refs_5_
  44.2 7.0 %shard_map.89 = bf16[32,8,2048]{2,1,0:T(8,128)(2,1)} custom-call(bf16[32,8,2048]{2,1,0:T(8,128)(2,1)S(1)} %all-to-all-done.x_ref, bf16[224,4096]{1,0:T(8,128)(2,1)S(1)} %bitcast.8, bf16[224,4096]{1,0:T(8,128)(2,1)} %collective-permute-done.3.refs_1_, bf16[224,4096]{1,0:T(8,128)(2,1)} %bitcast.10, bf16[224,4096]{1,0:T(8,128)(2,1)} %collective-permute-done.4.refs_3_, ...), custom_call_target="tpu_custom_call" | custom-call | flops 1409286144 | bytes 12845056 | tf_op jit(solution)/shard_map/pallas_call | solution.py:24
  51.2 0.0 copy-start.7
  51.2 0.0 copy-start.5
  51.2 0.0 copy-start.2
  51.2 0.0 copy-start.3
  51.2 8.2 %all-to-all-start.1 = ((bf16[16,16,2048]{2,1,0:T(8,128)(2,1)}), bf16[16,16,2048]{2,1,0:T(8,128)(2,1)S(1)}, u32[]{:S(2)}, u32[]{:S(2)}) async-start(bf16[16,16,2048]{2,1,0:T(8,128)(2,1)} %bitcast.6), calls=%async_computation.1 | async-start | bytes 2097152 | tf_op jit(solution)/shard_map/all_to_all | solution.py:214
  59.4 0.0 copy-done.7
  59.4 11.9 %collective-permute-start.6 = (bf16[256,128]{1,0:T(8,128)(2,1)S(1)}, bf16[256,128]{1,0:T(8,128)(2,1)S(1)}, u32[]{:S(2)}, u32[]{:S(2)}) collective-permute-start(bf16[256,128]{1,0:T(8,128)(2,1)S(1)} %copy-done.7), channel_id=1, source_target_pairs={{0,128},{64,0},{128,64},{1,129},{65,1},{129,65},{2,130},{66,2},{13... | collective-permute-start | bytes 196616 | tf_op jit(solution)/shard_map/ppermute | solution.py:158
  71.3 0.0 copy-done.5
  71.3 1.9 %collective-permute-start.8 = (bf16[256,128]{1,0:T(8,128)(2,1)S(1)}, bf16[256,128]{1,0:T(8,128)(2,1)S(1)}, u32[]{:S(2)}, u32[]{:S(2)}) collective-permute-start(bf16[256,128]{1,0:T(8,128)(2,1)S(1)} %copy-done.5), channel_id=1, source_target_pairs={{0,64},{64,128},{128,0},{1,65},{65,129},{129,1},{2,66},{66,130},{1... | collective-permute-start | bytes 196616 | tf_op jit(solution)/shard_map/ppermute | solution.py:158
  73.2 10.6 %all-to-all-done.1.in_ref = bf16[16,16,2048]{2,1,0:T(8,128)(2,1)S(1)} async-done(((bf16[16,16,2048]{2,1,0:T(8,128)(2,1)}), bf16[16,16,2048]{2,1,0:T(8,128)(2,1)S(1)}, u32[]{:S(2)}, u32[]{:S(2)}) %all-to-all-start.1) | async-done | bytes 1048608 | tf_op jit(solution)/shard_map/all_to_all | solution.py:214
  83.8 0.1 shard_map.90
  83.9 5.3 %collective-permute-done.6.refs_2_ = bf16[256,128]{1,0:T(8,128)(2,1)S(1)} collective-permute-done((bf16[256,128]{1,0:T(8,128)(2,1)S(1)}, bf16[256,128]{1,0:T(8,128)(2,1)S(1)}, u32[]{:S(2)}, u32[]{:S(2)}) %collective-permute-start.6) | collective-permute-done | bytes 65568 | tf_op jit(solution)/shard_map/ppermute | solution.py:158
  89.3 6.4 %collective-permute-start.7 = (bf16[8,2048]{1,0:T(8,128)(2,1)S(1)}, bf16[8,2048]{1,0:T(8,128)(2,1)S(1)}, u32[]{:S(2)}, u32[]{:S(2)}) collective-permute-start(bf16[8,2048]{1,0:T(8,128)(2,1)S(1)} %get-tuple-element.32), channel_id=1, source_target_pairs={{0,4},{4,0},{1,5},{5,1},{2,6},{6,2},{3,7},{7,3},{8,12},{12,8},{9,1... | collective-permute-start | bytes 98312 | tf_op jit(solution)/shard_map/ppermute | solution.py:158
  95.7 0.0 collective-permute-done.8.refs_1_
  95.7 0.7 shard_map.92
  96.4 1.2 %collective-permute-done.7.come_ref = bf16[8,2048]{1,0:T(8,128)(2,1)S(1)} collective-permute-done((bf16[8,2048]{1,0:T(8,128)(2,1)S(1)}, bf16[8,2048]{1,0:T(8,128)(2,1)S(1)}, u32[]{:S(2)}, u32[]{:S(2)}) %collective-permute-start.7) | collective-permute-done | bytes 32800 | tf_op jit(solution)/shard_map/ppermute | solution.py:158
  97.6 0.0 copy-done.2
  97.6 0.0 copy-done.3
  97.6 0.6 shard_map.91
Async XLA Ops:
  0.6 19.4 %copy-start = (bf16[4096,224]{0,1:T(8,128)(2,1)S(1)}, bf16[4096,224]{0,1:T(8,128)(2,1)}, u32[]{:S(2)}) copy-start(bf16[4096,224]{0,1:T(8,128)(2,1)} %param.9) | copy-start | bytes 5505028
  2.8 41.4 %all-to-all-start = ((bf16[32,8,2048]{2,1,0:T(8,128)(2,1)}), bf16[32,8,2048]{2,1,0:T(8,128)(2,1)S(1)}, u32[]{:S(2)}, u32[]{:S(2)}) async-start(bf16[32,8,2048]{2,1,0:T(8,128)(2,1)} %shard_map.86), calls=%async_computation | async-start | bytes 2097152 | tf_op jit(solution)/shard_map/all_to_all | solution.py:197
  16.6 8.2 %collective-permute-start = (bf16[256,384]{1,0:T(8,128)(2,1)}, bf16[256,384]{1,0:T(8,128)(2,1)S(1)}, u32[]{:S(2)}, u32[]{:S(2)}) collective-permute-start(bf16[256,384]{1,0:T(8,128)(2,1)} %get-tuple-element.20), channel_id=1, source_target_pairs={{0,192},{192,384},{384,576},{576,0},{1,193},{193,385},{385,577},{5... | collective-permute-start | bytes 589832 | tf_op jit(solution)/shard_map/ppermute | solution.py:158
  20.0 24.2 %collective-permute-start.3 = (bf16[224,4096]{1,0:T(8,128)(2,1)S(1)}, bf16[224,4096]{1,0:T(8,128)(2,1)}, u32[]{:S(2)}, u32[]{:S(2)}) collective-permute-start(bf16[224,4096]{1,0:T(8,128)(2,1)S(1)} %bitcast.7), channel_id=1, source_target_pairs={{0,1},{1,0},{2,3},{3,2},{4,5},{5,4},{6,7},{7,6},{8,9},{9,8},{10,11... | collective-permute-start | bytes 5505032 | tf_op jit(solution)/shard_map/ppermute | solution.py:158
  21.9 22.2 %collective-permute-start.4 = (bf16[224,4096]{1,0:T(8,128)(2,1)}, bf16[224,4096]{1,0:T(8,128)(2,1)}, u32[]{:S(2)}, u32[]{:S(2)}) collective-permute-start(bf16[224,4096]{1,0:T(8,128)(2,1)} %bitcast.9), channel_id=1, source_target_pairs={{0,1},{1,0},{2,3},{3,2},{4,5},{5,4},{6,7},{7,6},{8,9},{9,8},{10,11... | collective-permute-start | bytes 5505032 | tf_op jit(solution)/shard_map/ppermute | solution.py:158
  24.8 19.4 %collective-permute-start.5 = (bf16[224,4096]{1,0:T(8,128)(2,1)}, bf16[224,4096]{1,0:T(8,128)(2,1)}, u32[]{:S(2)}, u32[]{:S(2)}) collective-permute-start(bf16[224,4096]{1,0:T(8,128)(2,1)} %refs_4_), channel_id=1, source_target_pairs={{0,1},{1,0},{2,3},{3,2},{4,5},{5,4},{6,7},{7,6},{8,9},{9,8},{10,11... | collective-permute-start | bytes 5505032 | tf_op jit(solution)/shard_map/ppermute | solution.py:158
  26.7 11.3 %collective-permute-start.1 = (bf16[256,384]{1,0:T(8,128)(2,1)}, bf16[256,384]{1,0:T(8,128)(2,1)S(1)}, u32[]{:S(2)}, u32[]{:S(2)}) collective-permute-start(bf16[256,384]{1,0:T(8,128)(2,1)} %get-tuple-element.22), channel_id=1, source_target_pairs={{0,384},{192,576},{384,0},{576,192},{1,385},{193,577},{385,1},{577... | collective-permute-start | bytes 589832 | tf_op jit(solution)/shard_map/ppermute | solution.py:158
  30.7 11.1 %collective-permute-start.2 = (bf16[256,384]{1,0:T(8,128)(2,1)}, bf16[256,384]{1,0:T(8,128)(2,1)S(1)}, u32[]{:S(2)}, u32[]{:S(2)}) collective-permute-start(bf16[256,384]{1,0:T(8,128)(2,1)} %get-tuple-element.23), channel_id=1, source_target_pairs={{0,576},{192,0},{384,192},{576,384},{1,577},{193,1},{385,193},{577... | collective-permute-start | bytes 589832 | tf_op jit(solution)/shard_map/ppermute | solution.py:158
  41.8 0.9 copy-start.1
  42.9 0.6 copy-start.4
  43.5 0.6 copy-start.6
  51.2 8.2 %copy-start.7 = (bf16[256,128]{1,0:T(8,128)(2,1)S(1)}, bf16[256,128]{1,0:T(8,128)(2,1)}, u32[]{:S(2)}) copy-start(bf16[256,128]{1,0:T(8,128)(2,1)} %copy-done.6) | copy-start | bytes 196612
  51.2 20.1 %copy-start.5 = (bf16[256,128]{1,0:T(8,128)(2,1)S(1)}, bf16[256,128]{1,0:T(8,128)(2,1)}, u32[]{:S(2)}) copy-start(bf16[256,128]{1,0:T(8,128)(2,1)} %copy-done.4) | copy-start | bytes 196612
  51.2 46.3 %copy-start.2 = (bf16[4,4096]{1,0:T(4,128)(2,1)S(1)}, bf16[4,4096]{1,0:T(4,128)(2,1)}, u32[]{:S(2)}) copy-start(bf16[4,4096]{1,0:T(4,128)(2,1)} %tok_ref.1) | copy-start | bytes 98308
  51.2 46.3 %copy-start.3 = (s32[4,4096]{1,0:T(4,128)S(1)}, s32[4,4096]{1,0:T(4,128)}, u32[]{:S(2)}) copy-start(s32[4,4096]{1,0:T(4,128)} %mask_ref.1) | copy-start | bytes 196612
  51.2 32.6 %all-to-all-start.1 = ((bf16[16,16,2048]{2,1,0:T(8,128)(2,1)}), bf16[16,16,2048]{2,1,0:T(8,128)(2,1)S(1)}, u32[]{:S(2)}, u32[]{:S(2)}) async-start(bf16[16,16,2048]{2,1,0:T(8,128)(2,1)} %bitcast.6), calls=%async_computation.1 | async-start | bytes 2097152 | tf_op jit(solution)/shard_map/all_to_all | solution.py:214
  59.4 29.9 %collective-permute-start.6 = (bf16[256,128]{1,0:T(8,128)(2,1)S(1)}, bf16[256,128]{1,0:T(8,128)(2,1)S(1)}, u32[]{:S(2)}, u32[]{:S(2)}) collective-permute-start(bf16[256,128]{1,0:T(8,128)(2,1)S(1)} %copy-done.7), channel_id=1, source_target_pairs={{0,128},{64,0},{128,64},{1,129},{65,1},{129,65},{2,130},{66,2},{13... | collective-permute-start | bytes 196616 | tf_op jit(solution)/shard_map/ppermute | solution.py:158
  71.3 24.4 %collective-permute-start.8 = (bf16[256,128]{1,0:T(8,128)(2,1)S(1)}, bf16[256,128]{1,0:T(8,128)(2,1)S(1)}, u32[]{:S(2)}, u32[]{:S(2)}) collective-permute-start(bf16[256,128]{1,0:T(8,128)(2,1)S(1)} %copy-done.5), channel_id=1, source_target_pairs={{0,64},{64,128},{128,0},{1,65},{65,129},{129,1},{2,66},{66,130},{1... | collective-permute-start | bytes 196616 | tf_op jit(solution)/shard_map/ppermute | solution.py:158
  89.3 8.3 %collective-permute-start.7 = (bf16[8,2048]{1,0:T(8,128)(2,1)S(1)}, bf16[8,2048]{1,0:T(8,128)(2,1)S(1)}, u32[]{:S(2)}, u32[]{:S(2)}) collective-permute-start(bf16[8,2048]{1,0:T(8,128)(2,1)S(1)} %get-tuple-element.32), channel_id=1, source_target_pairs={{0,4},{4,0},{1,5},{5,1},{2,6},{6,2},{3,7},{7,3},{8,12},{12,8},{9,1... | collective-permute-start | bytes 98312 | tf_op jit(solution)/shard_map/ppermute | solution.py:158

commit v6 on v5

--- a/solution.py
+++ b/solution.py
@@ -16,7 +16,7 @@
 KEEP = 0.9
 
 
-def call(body, outs, *args, smem=0, hbm=0, scratch=(), vmem=16, flops=0, moved=1 << 20):
+def call(body, outs, *args, smem=0, hbm=0, far_out=False, scratch=(), vmem=16, flops=0, moved=1 << 20):
     whole = pl.BlockSpec(memory_space=pltpu.VMEM)
     specs = [pl.BlockSpec(memory_space=pltpu.SMEM)] * smem
     specs += [whole] * (len(args) - smem - hbm)
@@ -25,7 +25,7 @@
         body,
         out_shape=outs,
         in_specs=specs,
-        out_specs=jax.tree.map(lambda _: whole, outs),
+        out_specs=jax.tree.map(lambda _: pl.BlockSpec(memory_space=pltpu.HBM) if far_out else whole, outs),
         scratch_shapes=list(scratch),
         compiler_params=pltpu.CompilerParams(vmem_limit_bytes=vmem << 20),
         cost_estimate=pl.CostEstimate(flops=flops, bytes_accessed=moved, transcendentals=0),
@@ -39,7 +39,7 @@
     return copies
 
 
-def norm_body(tok_hbm, gain_hbm, out_ref, tok_ref, gain_ref, sems):
+def norm_body(tok_hbm, gain_hbm, out_hbm, tok_ref, gain_ref, block_ref, sems, sent):
     half = tok_ref.shape[1] // 2
     for copy in brought(((tok_hbm, tok_ref), (gain_hbm, gain_ref)), sems):
         copy.wait()
@@ -47,8 +47,10 @@
     scale = lax.rsqrt(jnp.mean(inputs * inputs, axis=-1, keepdims=True) + EPS)
     normed = inputs * scale * gain_ref[...].astype(F32)[None, :]
     block = jnp.concatenate([normed[:, :half], normed[:, half:]], axis=0).astype(BF16)
-    for i in range(out_ref.shape[0]):
-        out_ref[i] = block
+    block_ref[...] = block
+    pairs = [(block_ref, out_hbm.at[i]) for i in range(out_hbm.shape[0])]
+    for copy in brought(pairs, sent):
+        copy.wait()
 
 
 def paired(first, second):
@@ -163,7 +165,7 @@
     nx = lax.axis_size("x")
     cut = call(
         cut_body, (shape(rows, cols // nx),) * nx, place("x"), bucket,
-        smem=1, hbm=1, vmem=60, scratch=[pltpu.SemaphoreType.DMA((nx,))],
+        smem=1, hbm=1, vmem=40, scratch=[pltpu.SemaphoreType.DMA((nx,))],
     )
     return [cut[0]] + [passed_on(cut[k], "x", k) for k in range(1, nx)]
 
@@ -187,11 +189,13 @@
 
     gathered = call(
         norm_body, blocks, tokens, norm_gain,
-        hbm=2, vmem=60,
+        hbm=2, vmem=60, far_out=True,
         scratch=[
             pltpu.VMEM(tokens.shape, BF16),
             pltpu.VMEM(norm_gain.shape, BF16),
+            pltpu.VMEM((2 * few, wide // 2), BF16),
             pltpu.SemaphoreType.DMA((2,)),
+            pltpu.SemaphoreType.DMA((chips,)),
         ],
     )
     gathered = lax.all_to_all(gathered, CHIPS, 0, 0, tiled=True)

time: 98.8 us -> 98.8 us (level)
  the two profiles are of different devices: /device:TPU:122 before, /device:TPU:126 now
where the time goes in v6:
time: 98.8 us; the launch traced here: 98.2 us
  starting transfers between devices  55 us (56%)
  waiting for transfers between devices  27.1 us (27%)
  Pallas kernels  12.8 us (13%)
  local copies, waits for them, and re-layouts  2.4 us (2%)
    ppermute x9, starting transfers between devices, passed_on(): return lax.ppermute(x, axis, [(i, (i + by) % size) for i in range(size)])  35.2 us
    ppermute x9, waiting for transfers between devices, passed_on(): return lax.ppermute(x, axis, [(i, (i + by) % size) for i in range(size)])  16.6 us
    pallas_call x7, Pallas kernels, call(): pl.pallas_call(body, out_shape=outs, in_specs=specs, out_specs=jax.tree.m...  12.8 us
    all_to_all x1, starting transfers between devices, per_device(): gathered = lax.all_to_all(gathered, CHIPS, 0, 0, tiled=True)  11.6 us
    all_to_all x1, waiting for transfers between devices, per_device(): terms = lax.all_to_all(terms, ('y', 'zb'), 0, 0, tiled=True)  10.6 us
    all_to_all x1, starting transfers between devices, per_device(): terms = lax.all_to_all(terms, ('y', 'zb'), 0, 0, tiled=True)  8.19 us
    unnamed x16, local copies, waits for them, and re-layouts  2.4 us
  transfers between devices with their start and end apart: 11, of which 6 were waited for; matrix products, arithmetic and copies ran while one was open for 0% of the time, Pallas kernels for 3%

profile of v6, /device:TPU:126, one launch (start us, length us, event | category | flops | bytes accessed | tf_op | source)
XLA Modules:
  0.0 98.2 jit_solution(11626357996901808053)
XLA Ops:
  0.6 0.0 copy-start
  0.6 2.3 %shard_map.86 = bf16[32,8,2048]{2,1,0:T(8,128)(2,1)} custom-call(bf16[4,4096]{1,0:T(4,128)(2,1)} %tok_ref.1, bf16[4096]{0:T(1024)(128)(2,1)} %gain_hbm.1), custom_call_target="tpu_custom_call" | custom-call | bytes 1048576 | tf_op jit(solution)/shard_map/pallas_call | solution.py:24
  3.0 11.6 %all-to-all-start = ((bf16[32,8,2048]{2,1,0:T(8,128)(2,1)}), bf16[32,8,2048]{2,1,0:T(8,128)(2,1)S(1)}, u32[]{:S(2)}, u32[]{:S(2)}) async-start(bf16[32,8,2048]{2,1,0:T(8,128)(2,1)} %shard_map.86), calls=%async_computation | async-start | bytes 2097152 | tf_op jit(solution)/shard_map/all_to_all | solution.py:201
  14.6 0.0 copy-start.1
  14.6 1.1 %copy-done.1 = bf16[1,256,1536]{2,1,0:T(8,128)(2,1)S(1)} copy-done((bf16[1,256,1536]{2,1,0:T(8,128)(2,1)S(1)}, bf16[1,256,1536]{2,1,0:T(8,128)(2,1)}, u32[]{:S(2)}) %copy-start.1) | copy-done | bytes 786456
  15.8 0.9 shard_map.87
  16.7 2.4 %collective-permute-start = (bf16[256,384]{1,0:T(8,128)(2,1)S(1)}, bf16[256,384]{1,0:T(8,128)(2,1)S(1)}, u32[]{:S(2)}, u32[]{:S(2)}) collective-permute-start(bf16[256,384]{1,0:T(8,128)(2,1)S(1)} %get-tuple-element.20), channel_id=1, source_target_pairs={{0,192},{192,384},{384,576},{576,0},{1,193},{193,385},{385,577},{5... | collective-permute-start | bytes 589832 | tf_op jit(solution)/shard_map/ppermute | solution.py:160
  19.1 0.0 copy-done
  19.1 1.9 %collective-permute-start.3 = (bf16[224,4096]{1,0:T(8,128)(2,1)S(1)}, bf16[224,4096]{1,0:T(8,128)(2,1)}, u32[]{:S(2)}, u32[]{:S(2)}) collective-permute-start(bf16[224,4096]{1,0:T(8,128)(2,1)S(1)} %bitcast.7), channel_id=1, source_target_pairs={{0,1},{1,0},{2,3},{3,2},{4,5},{5,4},{6,7},{7,6},{8,9},{9,8},{10,11... | collective-permute-start | bytes 5505032 | tf_op jit(solution)/shard_map/ppermute | solution.py:160
  21.0 2.4 %collective-permute-start.4 = (bf16[224,4096]{1,0:T(8,128)(2,1)}, bf16[224,4096]{1,0:T(8,128)(2,1)}, u32[]{:S(2)}, u32[]{:S(2)}) collective-permute-start(bf16[224,4096]{1,0:T(8,128)(2,1)} %bitcast.10), channel_id=1, source_target_pairs={{0,1},{1,0},{2,3},{3,2},{4,5},{5,4},{6,7},{7,6},{8,9},{9,8},{10,11... | collective-permute-start | bytes 5505032 | tf_op jit(solution)/shard_map/ppermute | solution.py:160
  23.4 1.2 %collective-permute-done.refs_1_ = bf16[256,384]{1,0:T(8,128)(2,1)S(1)} collective-permute-done((bf16[256,384]{1,0:T(8,128)(2,1)S(1)}, bf16[256,384]{1,0:T(8,128)(2,1)S(1)}, u32[]{:S(2)}, u32[]{:S(2)}) %collective-permute-start) | collective-permute-done | bytes 196640 | tf_op jit(solution)/shard_map/ppermute | solution.py:160
  24.6 1.9 %collective-permute-start.5 = (bf16[224,4096]{1,0:T(8,128)(2,1)}, bf16[224,4096]{1,0:T(8,128)(2,1)}, u32[]{:S(2)}, u32[]{:S(2)}) collective-permute-start(bf16[224,4096]{1,0:T(8,128)(2,1)} %refs_4_), channel_id=1, source_target_pairs={{0,1},{1,0},{2,3},{3,2},{4,5},{5,4},{6,7},{7,6},{8,9},{9,8},{10,11... | collective-permute-start | bytes 5505032 | tf_op jit(solution)/shard_map/ppermute | solution.py:160
  26.6 3.3 %collective-permute-start.1 = (bf16[256,384]{1,0:T(8,128)(2,1)}, bf16[256,384]{1,0:T(8,128)(2,1)S(1)}, u32[]{:S(2)}, u32[]{:S(2)}) collective-permute-start(bf16[256,384]{1,0:T(8,128)(2,1)} %get-tuple-element.22), channel_id=1, source_target_pairs={{0,384},{192,576},{384,0},{576,192},{1,385},{193,577},{385,1},{577... | collective-permute-start | bytes 589832 | tf_op jit(solution)/shard_map/ppermute | solution.py:160
  29.9 3.0 %collective-permute-start.2 = (bf16[256,384]{1,0:T(8,128)(2,1)}, bf16[256,384]{1,0:T(8,128)(2,1)}, u32[]{:S(2)}, u32[]{:S(2)}) collective-permute-start(bf16[256,384]{1,0:T(8,128)(2,1)} %get-tuple-element.23), channel_id=1, source_target_pairs={{0,576},{192,0},{384,192},{576,384},{1,577},{193,1},{385,193},{577... | collective-permute-start | bytes 589832 | tf_op jit(solution)/shard_map/ppermute | solution.py:160
  32.9 4.9 %collective-permute-done.1.refs_2_ = bf16[256,384]{1,0:T(8,128)(2,1)S(1)} collective-permute-done((bf16[256,384]{1,0:T(8,128)(2,1)}, bf16[256,384]{1,0:T(8,128)(2,1)S(1)}, u32[]{:S(2)}, u32[]{:S(2)}) %collective-permute-start.1) | collective-permute-done | bytes 196640 | tf_op jit(solution)/shard_map/ppermute | solution.py:160
  37.9 3.9 %collective-permute-done.2.refs_3_ = bf16[256,384]{1,0:T(8,128)(2,1)} collective-permute-done((bf16[256,384]{1,0:T(8,128)(2,1)}, bf16[256,384]{1,0:T(8,128)(2,1)}, u32[]{:S(2)}, u32[]{:S(2)}) %collective-permute-start.2) | collective-permute-done | bytes 196640 | tf_op jit(solution)/shard_map/ppermute | solution.py:160
  41.8 1.1 %shard_map.88 = (bf16[256,128]{1,0:T(8,128)(2,1)S(1)}, bf16[256,128]{1,0:T(8,128)(2,1)S(1)}, bf16[256,128]{1,0:T(8,128)(2,1)S(1)}) custom-call(s32[1]{0:T(128)} %bitcast.1.place_ref, bf16[256,384]{1,0:T(8,128)(2,1)S(1)} %get-tuple-element.19.refs_0_, bf16[256,384]{1,0:T(8,128)(2,1)S(1)} %collective-permute-done.refs_1_, ...), custom_call_target="tpu_custom_call" | custom-call | bytes 1048576 | tf_op jit(solution)/shard_map/pallas_call | solution.py:24
  42.9 0.0 copy-start.4
  42.9 0.6 copy-done.4
  43.5 0.0 copy-start.6
  43.5 0.6 copy-done.6
  44.1 0.0 all-to-all-done.x_ref
  44.1 0.0 collective-permute-done.3.refs_1_
  44.1 0.0 collective-permute-done.4.refs_3_
  44.1 0.0 collective-permute-done.5.refs_5_
  44.1 7.0 %shard_map.89 = bf16[32,8,2048]{2,1,0:T(8,128)(2,1)} custom-call(bf16[32,8,2048]{2,1,0:T(8,128)(2,1)S(1)} %all-to-all-done.x_ref, bf16[224,4096]{1,0:T(8,128)(2,1)S(1)} %bitcast.8, bf16[224,4096]{1,0:T(8,128)(2,1)} %collective-permute-done.3.refs_1_, bf16[224,4096]{1,0:T(8,128)(2,1)} %bitcast.11, bf16[224,4096]{1,0:T(8,128)(2,1)} %collective-permute-done.4.refs_3_, ...), custom_call_target="tpu_custom_call" | custom-call | flops 1409286144 | bytes 12845056 | tf_op jit(solution)/shard_map/pallas_call | solution.py:24
  51.2 0.0 copy-start.7
  51.2 0.0 copy-start.5
  51.2 0.0 copy-start.2
  51.2 0.0 copy-start.3
  51.2 8.2 %all-to-all-start.1 = ((bf16[16,16,2048]{2,1,0:T(8,128)(2,1)}), bf16[16,16,2048]{2,1,0:T(8,128)(2,1)S(1)}, u32[]{:S(2)}, u32[]{:S(2)}) async-start(bf16[16,16,2048]{2,1,0:T(8,128)(2,1)} %bitcast.6), calls=%async_computation.1 | async-start | bytes 2097152 | tf_op jit(solution)/shard_map/all_to_all | solution.py:218
  59.4 0.0 copy-done.7
  59.4 11.9 %collective-permute-start.6 = (bf16[256,128]{1,0:T(8,128)(2,1)S(1)}, bf16[256,128]{1,0:T(8,128)(2,1)S(1)}, u32[]{:S(2)}, u32[]{:S(2)}) collective-permute-start(bf16[256,128]{1,0:T(8,128)(2,1)S(1)} %copy-done.7), channel_id=1, source_target_pairs={{0,128},{64,0},{128,64},{1,129},{65,1},{129,65},{2,130},{66,2},{13... | collective-permute-start | bytes 196616 | tf_op jit(solution)/shard_map/ppermute | solution.py:160
  71.3 0.0 copy-done.5
  71.3 1.9 %collective-permute-start.8 = (bf16[256,128]{1,0:T(8,128)(2,1)S(1)}, bf16[256,128]{1,0:T(8,128)(2,1)S(1)}, u32[]{:S(2)}, u32[]{:S(2)}) collective-permute-start(bf16[256,128]{1,0:T(8,128)(2,1)S(1)} %copy-done.5), channel_id=1, source_target_pairs={{0,64},{64,128},{128,0},{1,65},{65,129},{129,1},{2,66},{66,130},{1... | collective-permute-start | bytes 196616 | tf_op jit(solution)/shard_map/ppermute | solution.py:160
  73.2 10.6 %all-to-all-done.1.in_ref = bf16[16,16,2048]{2,1,0:T(8,128)(2,1)S(1)} async-done(((bf16[16,16,2048]{2,1,0:T(8,128)(2,1)}), bf16[16,16,2048]{2,1,0:T(8,128)(2,1)S(1)}, u32[]{:S(2)}, u32[]{:S(2)}) %all-to-all-start.1) | async-done | bytes 1048608 | tf_op jit(solution)/shard_map/all_to_all | solution.py:218
  83.8 0.1 shard_map.90
  83.9 5.3 %collective-permute-done.6.refs_2_ = bf16[256,128]{1,0:T(8,128)(2,1)S(1)} collective-permute-done((bf16[256,128]{1,0:T(8,128)(2,1)S(1)}, bf16[256,128]{1,0:T(8,128)(2,1)S(1)}, u32[]{:S(2)}, u32[]{:S(2)}) %collective-permute-start.6) | collective-permute-done | bytes 65568 | tf_op jit(solution)/shard_map/ppermute | solution.py:160
  89.3 6.4 %collective-permute-start.7 = (bf16[8,2048]{1,0:T(8,128)(2,1)S(1)}, bf16[8,2048]{1,0:T(8,128)(2,1)S(1)}, u32[]{:S(2)}, u32[]{:S(2)}) collective-permute-start(bf16[8,2048]{1,0:T(8,128)(2,1)S(1)} %get-tuple-element.32), channel_id=1, source_target_pairs={{0,4},{4,0},{1,5},{5,1},{2,6},{6,2},{3,7},{7,3},{8,12},{12,8},{9,1... | collective-permute-start | bytes 98312 | tf_op jit(solution)/shard_map/ppermute | solution.py:160
  95.6 0.0 collective-permute-done.8.refs_1_
  95.6 0.7 shard_map.92
  96.3 1.2 %collective-permute-done.7.come_ref = bf16[8,2048]{1,0:T(8,128)(2,1)S(1)} collective-permute-done((bf16[8,2048]{1,0:T(8,128)(2,1)S(1)}, bf16[8,2048]{1,0:T(8,128)(2,1)S(1)}, u32[]{:S(2)}, u32[]{:S(2)}) %collective-permute-start.7) | collective-permute-done | bytes 32800 | tf_op jit(solution)/shard_map/ppermute | solution.py:160
  97.5 0.0 copy-done.2
  97.5 0.0 copy-done.3
  97.5 0.6 shard_map.91
Async XLA Ops:
  0.6 18.4 %copy-start = (bf16[4096,224]{0,1:T(8,128)(2,1)S(1)}, bf16[4096,224]{0,1:T(8,128)(2,1)}, u32[]{:S(2)}) copy-start(bf16[4096,224]{0,1:T(8,128)(2,1)} %param.9) | copy-start | bytes 5505028
  3.0 41.1 %all-to-all-start = ((bf16[32,8,2048]{2,1,0:T(8,128)(2,1)}), bf16[32,8,2048]{2,1,0:T(8,128)(2,1)S(1)}, u32[]{:S(2)}, u32[]{:S(2)}) async-start(bf16[32,8,2048]{2,1,0:T(8,128)(2,1)} %shard_map.86), calls=%async_computation | async-start | bytes 2097152 | tf_op jit(solution)/shard_map/all_to_all | solution.py:201
  14.6 1.1 %copy-start.1 = (bf16[1,256,1536]{2,1,0:T(8,128)(2,1)S(1)}, bf16[1,256,1536]{2,1,0:T(8,128)(2,1)}, u32[]{:S(2)}) copy-start(bf16[1,256,1536]{2,1,0:T(8,128)(2,1)} %param.13) | copy-start | bytes 2359300
  16.7 8.0 %collective-permute-start = (bf16[256,384]{1,0:T(8,128)(2,1)S(1)}, bf16[256,384]{1,0:T(8,128)(2,1)S(1)}, u32[]{:S(2)}, u32[]{:S(2)}) collective-permute-start(bf16[256,384]{1,0:T(8,128)(2,1)S(1)} %get-tuple-element.20), channel_id=1, source_target_pairs={{0,192},{192,384},{384,576},{576,0},{1,193},{193,385},{385,577},{5... | collective-permute-start | bytes 589832 | tf_op jit(solution)/shard_map/ppermute | solution.py:160
  19.1 25.0 %collective-permute-start.3 = (bf16[224,4096]{1,0:T(8,128)(2,1)S(1)}, bf16[224,4096]{1,0:T(8,128)(2,1)}, u32[]{:S(2)}, u32[]{:S(2)}) collective-permute-start(bf16[224,4096]{1,0:T(8,128)(2,1)S(1)} %bitcast.7), channel_id=1, source_target_pairs={{0,1},{1,0},{2,3},{3,2},{4,5},{5,4},{6,7},{7,6},{8,9},{9,8},{10,11... | collective-permute-start | bytes 5505032 | tf_op jit(solution)/shard_map/ppermute | solution.py:160
  21.0 23.1 %collective-permute-start.4 = (bf16[224,4096]{1,0:T(8,128)(2,1)}, bf16[224,4096]{1,0:T(8,128)(2,1)}, u32[]{:S(2)}, u32[]{:S(2)}) collective-permute-start(bf16[224,4096]{1,0:T(8,128)(2,1)} %bitcast.10), channel_id=1, source_target_pairs={{0,1},{1,0},{2,3},{3,2},{4,5},{5,4},{6,7},{7,6},{8,9},{9,8},{10,11... | collective-permute-start | bytes 5505032 | tf_op jit(solution)/shard_map/ppermute | solution.py:160
  24.6 19.5 %collective-permute-start.5 = (bf16[224,4096]{1,0:T(8,128)(2,1)}, bf16[224,4096]{1,0:T(8,128)(2,1)}, u32[]{:S(2)}, u32[]{:S(2)}) collective-permute-start(bf16[224,4096]{1,0:T(8,128)(2,1)} %refs_4_), channel_id=1, source_target_pairs={{0,1},{1,0},{2,3},{3,2},{4,5},{5,4},{6,7},{7,6},{8,9},{9,8},{10,11... | collective-permute-start | bytes 5505032 | tf_op jit(solution)/shard_map/ppermute | solution.py:160
  26.6 11.3 %collective-permute-start.1 = (bf16[256,384]{1,0:T(8,128)(2,1)}, bf16[256,384]{1,0:T(8,128)(2,1)S(1)}, u32[]{:S(2)}, u32[]{:S(2)}) collective-permute-start(bf16[256,384]{1,0:T(8,128)(2,1)} %get-tuple-element.22), channel_id=1, source_target_pairs={{0,384},{192,576},{384,0},{576,192},{1,385},{193,577},{385,1},{577... | collective-permute-start | bytes 589832 | tf_op jit(solution)/shard_map/ppermute | solution.py:160
  29.9 11.9 %collective-permute-start.2 = (bf16[256,384]{1,0:T(8,128)(2,1)}, bf16[256,384]{1,0:T(8,128)(2,1)}, u32[]{:S(2)}, u32[]{:S(2)}) collective-permute-start(bf16[256,384]{1,0:T(8,128)(2,1)} %get-tuple-element.23), channel_id=1, source_target_pairs={{0,576},{192,0},{384,192},{576,384},{1,577},{193,1},{385,193},{577... | collective-permute-start | bytes 589832 | tf_op jit(solution)/shard_map/ppermute | solution.py:160
  42.9 0.6 copy-start.4
  43.5 0.6 copy-start.6
  51.2 8.2 %copy-start.7 = (bf16[256,128]{1,0:T(8,128)(2,1)S(1)}, bf16[256,128]{1,0:T(8,128)(2,1)}, u32[]{:S(2)}) copy-start(bf16[256,128]{1,0:T(8,128)(2,1)} %copy-done.6) | copy-start | bytes 196612
  51.2 20.1 %copy-start.5 = (bf16[256,128]{1,0:T(8,128)(2,1)S(1)}, bf16[256,128]{1,0:T(8,128)(2,1)}, u32[]{:S(2)}) copy-start(bf16[256,128]{1,0:T(8,128)(2,1)} %copy-done.4) | copy-start | bytes 196612
  51.2 46.3 %copy-start.2 = (bf16[4,4096]{1,0:T(4,128)(2,1)S(1)}, bf16[4,4096]{1,0:T(4,128)(2,1)}, u32[]{:S(2)}) copy-start(bf16[4,4096]{1,0:T(4,128)(2,1)} %tok_ref.1) | copy-start | bytes 98308
  51.2 46.3 %copy-start.3 = (s32[4,4096]{1,0:T(4,128)S(1)}, s32[4,4096]{1,0:T(4,128)}, u32[]{:S(2)}) copy-start(s32[4,4096]{1,0:T(4,128)} %mask_ref.1) | copy-start | bytes 196612
  51.2 32.6 %all-to-all-start.1 = ((bf16[16,16,2048]{2,1,0:T(8,128)(2,1)}), bf16[16,16,2048]{2,1,0:T(8,128)(2,1)S(1)}, u32[]{:S(2)}, u32[]{:S(2)}) async-start(bf16[16,16,2048]{2,1,0:T(8,128)(2,1)} %bitcast.6), calls=%async_computation.1 | async-start | bytes 2097152 | tf_op jit(solution)/shard_map/all_to_all | solution.py:218
  59.4 29.9 %collective-permute-start.6 = (bf16[256,128]{1,0:T(8,128)(2,1)S(1)}, bf16[256,128]{1,0:T(8,128)(2,1)S(1)}, u32[]{:S(2)}, u32[]{:S(2)}) collective-permute-start(bf16[256,128]{1,0:T(8,128)(2,1)S(1)} %copy-done.7), channel_id=1, source_target_pairs={{0,128},{64,0},{128,64},{1,129},{65,1},{129,65},{2,130},{66,2},{13... | collective-permute-start | bytes 196616 | tf_op jit(solution)/shard_map/ppermute | solution.py:160
  71.3 24.4 %collective-permute-start.8 = (bf16[256,128]{1,0:T(8,128)(2,1)S(1)}, bf16[256,128]{1,0:T(8,128)(2,1)S(1)}, u32[]{:S(2)}, u32[]{:S(2)}) collective-permute-start(bf16[256,128]{1,0:T(8,128)(2,1)S(1)} %copy-done.5), channel_id=1, source_target_pairs={{0,64},{64,128},{128,0},{1,65},{65,129},{129,1},{2,66},{66,130},{1... | collective-permute-start | bytes 196616 | tf_op jit(solution)/shard_map/ppermute | solution.py:160
  89.3 8.3 %collective-permute-start.7 = (bf16[8,2048]{1,0:T(8,128)(2,1)S(1)}, bf16[8,2048]{1,0:T(8,128)(2,1)S(1)}, u32[]{:S(2)}, u32[]{:S(2)}) collective-permute-start(bf16[8,2048]{1,0:T(8,128)(2,1)S(1)} %get-tuple-element.32), channel_id=1, source_target_pairs={{0,4},{4,0},{1,5},{5,1},{2,6},{6,2},{3,7},{7,3},{8,12},{12,8},{9,1... | collective-permute-start | bytes 98312 | tf_op jit(solution)/shard_map/ppermute | solution.py:160
